TPU v7x, 32 devices: a whole 2x2x4 slice. The times are simulated.
32 devices in a mesh: seq: 8 (over y, x, core), head: 4 (over z).
Axes of the slice: x: 2, y: 2, z: 4, core: 2. Of those that a mesh axis runs over, the one named last changes fastest.
Arguments:
- queries: bfloat16 [4096, 4096], P('seq', 'head'), may hold values from -15 to 15
- keys: bfloat16 [4096, 2048], P('seq', 'head'), may hold values from -6 to 6
- values: bfloat16 [4096, 2048], P('seq', 'head'), may hold values from -6 to 6
- out_grad: bfloat16 [4096, 4096], P('seq', 'head'), may hold values from -48 to 48
- normed: bfloat16 [4096, 4608], P('seq'), may hold values from -1.1953125 to 1.1953125
- w_query: bfloat16 [4608, 4096], P(None, 'head'), may hold values from -0.125 to 0.125
- w_key: bfloat16 [4608, 2048], P(None, 'head'), may hold values from -0.125 to 0.125
- w_value: bfloat16 [4608, 2048], P(None, 'head'), may hold values from -0.125 to 0.125
- valid_len: int32 [8], replicated, may hold values from 128 to 512, as said below
Outputs:
- grad_x: bfloat16 [4096, 4608], P('seq', 'head')
- grad_wq: bfloat16 [4608, 4096], P('seq', 'head')
- grad_wk: bfloat16 [4608, 2048], P('seq', 'head')
- grad_wv: bfloat16 [4608, 2048], P('seq', 'head')
Inputs may be any that keep to these rules, and one draw needn't show every extreme that they name: `valid_len`: every entry lies between 128 and 512; some shard is full and some shard has exactly 128 live slots.
All inputs are finite; a program needn't handle non-finite values.
Results may differ from a plain program's by a relative error of at most 0.024.
Values may be sent and summed in bfloat16 or wider, within the bound.
No kernel may reach another device: no remote copies, remote signals or barrier semaphores. Data moves between devices by JAX's collectives and lax.ppermute only.
A program may use at most 256 MiB of HBM per device.

v0:
```python
import functools
import math

import jax
import jax.numpy as jnp
from jax import lax
from jax.experimental import pallas as pl
from jax.experimental.pallas import tpu as pltpu
from jax.sharding import PartitionSpec as P

D = 4608
H = 32
HD = 128
WINDOW = 4096


SOFT_CAP = 50.0
ROPE_BASE = 10000.0


def passed_along(value, axis, by):
    size = lax.axis_size(axis)
    pairs = [(i, i + by) for i in range(size) if 0 <= i + by < size]
    return lax.ppermute(value, axis, pairs)


def rotate_back(gradient, positions, head_count):
    row_count = gradient.shape[0]
    half_width = HD // 2
    inverse_freq = ROPE_BASE ** (-(jnp.arange(half_width, dtype=jnp.float32) * (2.0 / HD)))
    angles = positions.astype(jnp.float32)[:, None] * inverse_freq[None, :]
    cosine = jnp.cos(angles)[:, None, :]
    sine_part = jnp.sin(angles)[:, None, :]
    per_head = gradient.reshape(row_count, head_count, HD)
    leading = per_head[:, :, :half_width]
    trailing = per_head[:, :, half_width:]
    rotated = jnp.concatenate(
        [leading * cosine + trailing * sine_part, trailing * cosine - leading * sine_part], axis=2
    )
    return rotated.reshape(row_count, head_count * HD)


def times_t(left, right):
    return lax.dot_general(
        left, right, (((1,), (1,)), ((), ())), preferred_element_type=jnp.float32
    )


def inner_rows(left, right):
    return lax.dot_general(
        left, right, (((0,), (0,)), ((), ())), preferred_element_type=jnp.float32
    )


def general_body(queries, keys, values, out_grad, normed, w_query, w_key, w_value, valid_len):
    row_count = queries.shape[0]
    kv_heads = keys.shape[1] // HD
    head_count = queries.shape[1] // HD
    group_size = head_count // kv_heads
    kv_width = kv_heads * HD
    hop_count = WINDOW // row_count
    score_scale = (D // H) ** (-0.5)
    shard_index = lax.axis_index("seq")
    last_shard = valid_len.shape[0] - 1
    row_iota = jnp.arange(row_count, dtype=jnp.int32)
    query_pos = shard_index * row_count + row_iota
    own_valid = row_iota < valid_len[shard_index]
    grad_rows = jnp.where(own_valid[:, None], out_grad, jnp.zeros_like(out_grad))
    query_blocks = queries.reshape(row_count, kv_heads, group_size, HD)
    grad_blocks = grad_rows.reshape(row_count, kv_heads, group_size, HD)
    key_value = jnp.concatenate([keys, values], axis=1)
    arrived = [key_value]
    moving = key_value
    for distance in range(1, hop_count + 1):
        moving = passed_along(moving, "seq", 1)
        arrived.append(moving)
    allowed_list = []
    capped_list = []
    running = jnp.zeros((kv_heads, group_size, row_count), jnp.float32)
    for distance in range(hop_count + 1):
        key_pos = (shard_index - distance) * row_count + row_iota
        owner = jnp.clip(shard_index - distance, 0, last_shard)
        key_valid = row_iota < valid_len[owner]
        offset_gap = query_pos[:, None] - key_pos[None, :]
        allowed = (
            (offset_gap >= 0)
            & (offset_gap < WINDOW)
            & (key_pos[None, :] >= 0)
            & (key_valid[None, :] | (offset_gap == 0))
        )
        key_block = arrived[distance][:, :kv_width].reshape(row_count, kv_heads, HD)
        raw_scores = (
            jnp.einsum(
                "qhgd,khd->hgqk", query_blocks, key_block, preferred_element_type=jnp.float32
            )
            * score_scale
        )
        capped = SOFT_CAP * jnp.tanh(raw_scores / SOFT_CAP)
        running = running + jnp.sum(jnp.where(allowed, jnp.exp(capped), 0.0), axis=-1)
        allowed_list.append(allowed)
        capped_list.append(capped)
    log_total = jnp.log(running)[..., None]
    attended = jnp.zeros((row_count, kv_heads, group_size, HD), jnp.float32)
    for distance in range(hop_count + 1):
        value_block = arrived[distance][:, kv_width:].reshape(row_count, kv_heads, HD)
        rounded = jnp.where(
            allowed_list[distance], jnp.exp(capped_list[distance] - log_total), 0.0
        ).astype(jnp.bfloat16)
        attended = attended + jnp.einsum(
            "hgqk,khd->qhgd", rounded, value_block, preferred_element_type=jnp.float32
        )
    row_delta = jnp.sum(grad_blocks.astype(jnp.float32) * attended, axis=-1)
    delta_cols = jnp.transpose(row_delta, (1, 2, 0))[..., None]
    query_grad = jnp.zeros((row_count, kv_heads, group_size, HD), jnp.float32)
    partials = [None] * (hop_count + 1)
    for distance in range(hop_count, -1, -1):
        key_block = arrived[distance][:, :kv_width].reshape(row_count, kv_heads, HD)
        value_block = arrived[distance][:, kv_width:].reshape(row_count, kv_heads, HD)
        capped = capped_list[distance]
        exact = jnp.where(allowed_list[distance], jnp.exp(capped - log_total), 0.0)
        rounded = exact.astype(jnp.bfloat16)
        grad_probs = jnp.einsum(
            "qhgd,khd->hgqk", grad_blocks, value_block, preferred_element_type=jnp.float32
        )
        grad_scores = (exact * (grad_probs - delta_cols) * (1.0 - (capped / SOFT_CAP) ** 2)).astype(
            jnp.bfloat16
        )
        query_grad = (
            query_grad
            + jnp.einsum(
                "hgqk,khd->qhgd", grad_scores, key_block, preferred_element_type=jnp.float32
            )
            * score_scale
        )
        key_grad = (
            jnp.einsum(
                "hgqk,qhgd->khd", grad_scores, query_blocks, preferred_element_type=jnp.float32
            )
            * score_scale
        )
        value_grad = jnp.einsum(
            "hgqk,qhgd->khd", rounded, grad_blocks, preferred_element_type=jnp.float32
        )
        partials[distance] = jnp.concatenate(
            [key_grad.reshape(row_count, kv_width), value_grad.reshape(row_count, kv_width)], axis=1
        )
    carried = partials[hop_count]
    for distance in range(hop_count - 1, -1, -1):
        carried = (
            passed_along(carried.astype(jnp.bfloat16), "seq", -1).astype(carried.dtype)
            + partials[distance]
        )
    query_pre = rotate_back(
        query_grad.reshape(row_count, head_count * HD), query_pos, head_count
    ).astype(jnp.bfloat16)
    key_pre = rotate_back(carried[:, :kv_width], query_pos, kv_heads).astype(jnp.bfloat16)
    value_pre = carried[:, kv_width:].astype(jnp.bfloat16)
    input_terms = (
        times_t(query_pre, w_query) + times_t(key_pre, w_key) + times_t(value_pre, w_value)
    )
    grad_x = lax.psum_scatter(
        input_terms.astype(jnp.bfloat16), "head", scatter_dimension=1, tiled=True
    )
    stacked = jnp.concatenate([query_pre, key_pre, value_pre], axis=1)
    weight_total = lax.psum_scatter(
        inner_rows(normed, stacked).astype(jnp.bfloat16), "seq", scatter_dimension=0, tiled=True
    ).astype(jnp.float32)
    query_cols = head_count * HD
    grad_wq = weight_total[:, :query_cols].astype(jnp.bfloat16)
    grad_wk = weight_total[:, query_cols : query_cols + kv_width].astype(jnp.bfloat16)
    grad_wv = weight_total[:, query_cols + kv_width :].astype(jnp.bfloat16)
    return (grad_x, grad_wq, grad_wk, grad_wv)
QB = 512
KB = 512
PACK_ROWS = 128
SHARE_COLS = 384
MIB = 1024 * 1024
NT = (((1,), (1,)), ((), ()))
NN = (((1,), (0,)), ((), ()))


def dot(a, b, dims):
    return lax.dot_general(a, b, dims, preferred_element_type=jnp.float32)


def attention_kernel(shards, rows, score_scale, place, lens, *refs):
    n = shards
    qg_in, mine_in, peer_in = refs[:3]
    cos_r, sin_r, cos_s, sin_s = refs[3:7]
    dq_out, keep_out, give_out = refs[7:10]
    (q2, k2, kT, gx, vx, alive, probs, slopes, dps, dq, dk, dv, dqT, qT, gT, sems) = refs[10:]
    me = place[0]
    core = lax.rem(me, 2)
    copies = []
    mine_at = pl.ds(pl.multiple_of((2 + core) * HD, HD), HD)
    peer_at = pl.ds(pl.multiple_of((3 - core) * HD, HD), HD)
    for m in range(n):
        to = pl.ds(m * rows, rows)
        copies.append(pltpu.make_async_copy(qg_in.at[m], probs.at[to, pl.ds(0, 2 * HD)], sems.at[0, m]))
        copies.append(pltpu.make_async_copy(mine_in.at[m], probs.at[to, mine_at], sems.at[1, m]))
        copies.append(pltpu.make_async_copy(peer_in.at[m], probs.at[to, peer_at], sems.at[2, m]))
    for copy in copies:
        copy.start()
    dk[...] = jnp.zeros_like(dk)
    dv[...] = jnp.zeros_like(dv)
    for copy in copies:
        copy.wait()

    piece = 128
    lane = lax.broadcasted_iota(jnp.int32, (piece, HD), 1)

    def pack_shard(shard, offset):
        valid = lens[shard]

        def pack_piece(i, _):
            src = pl.multiple_of(i * piece, piece)
            dst = pl.multiple_of(offset + i * piece, 16)
            live = (lax.broadcasted_iota(jnp.int32, (piece, HD), 0) + src) < valid
            at = pl.ds(pl.multiple_of(shard * rows + src, piece), piece)
            to = pl.ds(dst, piece)
            q = jnp.where(live, probs[at, :HD].astype(jnp.float32), 0.0) * (score_scale / SOFT_CAP)
            hi = q.astype(jnp.bfloat16)
            q2[to, :HD] = hi
            q2[to, HD:] = (q - hi.astype(jnp.float32)).astype(jnp.bfloat16)
            zero = jnp.zeros((piece, HD), jnp.bfloat16)
            gx[to, :] = jnp.where(live, probs[at, HD : 2 * HD], zero)
            k = jnp.where(live, probs[at, 2 * HD : 3 * HD], zero)
            k2[to, :HD] = k
            k2[to, HD:] = k
            vx[to, :] = jnp.where(live, probs[at, 3 * HD : 4 * HD], zero)
            alive[to, :] = jnp.where(live, 1.0, 0.0)
            return 0

        lax.fori_loop(0, pl.cdiv(valid, piece), pack_piece, 0)
        return offset + ((valid + 15) // 16) * 16

    end = lax.fori_loop(0, n, pack_shard, jnp.int32(0))
    tail = pl.ds(pl.multiple_of(end, 16), KB)
    for ref in (q2, k2, gx, vx, alive):
        ref[tail, :] = jnp.zeros((KB, ref.shape[1]), ref.dtype)
    blocks = pl.cdiv(end, QB)

    def turn(i, _):
        at = pl.ds(pl.multiple_of(i * KB, KB), KB)
        kT[:, at] = k2[at, :HD].T
        return 0

    lax.fori_loop(0, pl.cdiv(end, KB), turn, 0)

    def block(b, _):
        first = pl.multiple_of(b * QB, QB)
        own = pl.ds(first, QB)
        qT[...] = q2[own, :].T
        gT[...] = gx[own, :].T
        dqT[...] = jnp.zeros_like(dqT)

        def forward(at, late, sums, masked):
            size = at.size
            t = jnp.tanh(dot(k2[at, :], qT[:, late:], NN))
            dp = dot(vx[at, :], gT[:, late:], NN)
            e = jnp.exp2(t * (SOFT_CAP * math.log2(math.e)))
            e = e * jnp.concatenate([alive[at, :]] * ((QB - late) // HD), axis=1)
            if masked:
                key = lax.broadcasted_iota(jnp.int32, e.shape, 0)
                query = lax.broadcasted_iota(jnp.int32, e.shape, 1)
                e = jnp.where(key <= query, e, 0.0)
            probs[at, late:] = e.astype(jnp.bfloat16)
            slopes[at, late:] = (e * (1.0 - t * t)).astype(jnp.bfloat16)
            dps[at, late:] = dp
            new = [jnp.sum(e, axis=0, keepdims=True), jnp.sum(e * dp, axis=0, keepdims=True)]
            if late:
                new = [jnp.concatenate([jnp.zeros((1, late), jnp.float32), x], axis=1) for x in new]
            return sums[0] + new[0], sums[1] + new[1]

        def chunk(c):
            return pl.ds(pl.multiple_of(c * KB, KB), KB)

        half = QB // 2
        early_keys = pl.ds(first, half)
        late_keys = pl.ds(pl.multiple_of(first + half, half), half)
        zero = jnp.zeros((1, QB), jnp.float32)
        sums = lax.fori_loop(0, b, lambda c, sums: forward(chunk(c), 0, sums, False), (zero, zero))
        sums = forward(early_keys, 0, sums, True)
        total, weighted = forward(late_keys, half, sums, True)
        inv = 1.0 / total
        delta = weighted * inv
        gs = (gT[...].astype(jnp.float32) * inv).astype(jnp.bfloat16).T
        q = qT[:HD, :].astype(jnp.float32) + qT[HD:, :].astype(jnp.float32)
        qs = (q * (inv * SOFT_CAP)).astype(jnp.bfloat16).T

        def backward(at, late):
            ds = slopes[at, late:] * (dps[at, late:] - delta[:, late:]).astype(jnp.bfloat16)
            dqT[:, late:] += dot(kT[:, at], ds, NN)
            dk[at, :] += dot(ds, qs[late:, :], NN)
            dv[at, :] += dot(probs[at, late:], gs[late:, :], NN)

        lax.fori_loop(0, b, lambda c, _: (backward(chunk(c), 0), 0)[1], 0)
        backward(early_keys, 0)
        backward(late_keys, half)
        dq[own, :] = (dqT[...] * (inv * score_scale)).T
        return 0

    lax.fori_loop(0, blocks, block, 0)

    def unpack(j, _):
        shard = place[1 + j]
        offset = lax.fori_loop(0, shard, lambda s, o: o + ((lens[s] + 15) // 16) * 16, jnp.int32(0))
        valid = lens[shard]
        ca, sa = cos_s[pl.ds(shard, 1), :], sin_s[pl.ds(shard, 1), :]

        swapped = j + 1 - 2 * lax.rem(j, 2)

        def unpack_piece(i, _):
            dst = pl.multiple_of(i * piece, piece)
            src = pl.ds(pl.multiple_of(offset + i * piece, 16), piece)
            live = (lax.broadcasted_iota(jnp.int32, (piece, HD), 0) + dst) < valid
            cb, sb = cos_r[pl.ds(dst, piece), :], sin_r[pl.ds(dst, piece), :]
            cosine = ca * cb - sa * sb
            sine = sa * cb + ca * sb
            sine = jnp.where(lane < HD // 2, sine, -sine)

            def rotate(x):
                return x * cosine + pltpu.roll(x, HD // 2, 1) * sine

            to = pl.ds(pl.multiple_of(j * rows + i * piece, piece), piece)
            dq_out[to, :] = jnp.where(live, rotate(dq[src, :]), 0.0).astype(jnp.bfloat16)
            key_part = jnp.where(live, rotate(dk[src, :]), 0.0)
            value_part = jnp.where(live, dv[src, :], 0.0)
            keep_out[to, :] = jnp.where(core == 0, key_part, value_part)
            to = pl.ds(pl.multiple_of(swapped * rows + i * piece, piece), piece)
            give_out[to, :] = jnp.where(core == 0, value_part, key_part).astype(jnp.bfloat16)
            return 0

        def clear_piece(i, _):
            to = pl.ds(pl.multiple_of(j * rows + i * piece, piece), piece)
            dq_out[to, :] = jnp.zeros((piece, HD), jnp.bfloat16)
            keep_out[to, :] = jnp.zeros((piece, HD), jnp.float32)
            to = pl.ds(pl.multiple_of(swapped * rows + i * piece, piece), piece)
            give_out[to, :] = jnp.zeros((piece, HD), jnp.bfloat16)
            return 0

        used = pl.cdiv(valid, piece)
        lax.fori_loop(0, used, unpack_piece, 0)
        lax.fori_loop(used, rows // piece, clear_piece, 0)
        return 0

    lax.fori_loop(0, n, unpack, 0)


def attention(place, lens, qg, mine, peer, tables, score_scale):
    n, rows = qg.shape[:2]
    tokens = n * rows
    room = tokens + KB
    bf, f32 = jnp.bfloat16, jnp.float32
    any_spec = pl.BlockSpec(memory_space=pl.ANY)
    smem = pl.BlockSpec(memory_space=pltpu.SMEM)
    vmem = pl.BlockSpec(memory_space=pltpu.VMEM)
    return pl.pallas_call(
        functools.partial(attention_kernel, n, rows, score_scale),
        out_shape=(
            jax.ShapeDtypeStruct((tokens, HD), bf),
            jax.ShapeDtypeStruct((tokens, HD), f32),
            jax.ShapeDtypeStruct((tokens, HD), bf),
        ),
        in_specs=[smem, smem] + [any_spec] * 3 + [vmem] * 4,
        out_specs=(vmem, vmem, vmem),
        scratch_shapes=[
            pltpu.VMEM((room, 2 * HD), bf),
            pltpu.VMEM((room, 2 * HD), bf),
            pltpu.VMEM((HD, room), bf),
            pltpu.VMEM((room, HD), bf),
            pltpu.VMEM((room, HD), bf),
            pltpu.VMEM((room, HD), f32),
            pltpu.VMEM((room, QB), bf),
            pltpu.VMEM((room, QB), bf),
            pltpu.VMEM((room, QB), f32),
            pltpu.VMEM((room, HD), f32),
            pltpu.VMEM((room, HD), f32),
            pltpu.VMEM((room, HD), f32),
            pltpu.VMEM((HD, QB), f32),
            pltpu.VMEM((2 * HD, QB), bf),
            pltpu.VMEM((HD, QB), bf),
            pltpu.SemaphoreType.DMA((3, n)),
        ],
        compiler_params=pltpu.CompilerParams(vmem_limit_bytes=42 * MIB),
        cost_estimate=pl.CostEstimate(
            flops=12 * tokens * tokens * HD, bytes_accessed=16 * tokens * HD, transcendentals=tokens * tokens
        ),
        name="attention",
    )(place, lens, qg, mine, peer, *tables)


def tables(rows, shards):
    half = HD // 2
    freq = 10000.0 ** (-(jnp.arange(half, dtype=jnp.float32) * (2.0 / HD)))
    freq = jnp.concatenate([freq, freq])[None, :]
    within = jnp.arange(rows, dtype=jnp.float32)[:, None] * freq
    start = (jnp.arange(shards, dtype=jnp.float32) * rows)[:, None] * freq
    return jnp.cos(within), jnp.sin(within), jnp.cos(start), jnp.sin(start)


def pack_kernel(q, k, v, g, qg, kv, sems):
    n = qg.shape[0]
    copies = []
    for to in range(n):
        cols, kv_cols = pl.ds(to * HD, HD), pl.ds((to // 2) * HD, HD)
        copies.append(pltpu.make_async_copy((k, v)[to % 2].at[:, kv_cols], kv.at[to], sems.at[0, to]))
        copies.append(pltpu.make_async_copy(q.at[:, cols], qg.at[to, :, pl.ds(0, HD)], sems.at[1, to]))
        copies.append(pltpu.make_async_copy(g.at[:, cols], qg.at[to, :, pl.ds(HD, HD)], sems.at[2, to]))
    for copy in copies:
        copy.start()
    for copy in copies:
        copy.wait()


def pack(q, k, v, g, n):
    rows = q.shape[0]
    vmem = pl.BlockSpec(memory_space=pltpu.VMEM)
    return pl.pallas_call(
        pack_kernel,
        out_shape=(jax.ShapeDtypeStruct((n, rows, 2 * HD), q.dtype), jax.ShapeDtypeStruct((n, rows, HD), q.dtype)),
        in_specs=[pl.BlockSpec(memory_space=pltpu.HBM)] * 4,
        out_specs=(vmem, vmem),
        scratch_shapes=[pltpu.SemaphoreType.DMA((3, n))],
        compiler_params=pltpu.CompilerParams(vmem_limit_bytes=60 * MIB),
        name="pack",
    )(q, k, v, g)


def line_up_kernel(place, *refs):
    n = (len(refs) - 4) // 2
    for parts, out, theirs in ((refs[:n], refs[-4], refs[-2]), (refs[n : 2 * n], refs[-3], refs[-1])):
        rows = theirs.shape[0]
        for m, src in enumerate(parts):
            chip = place[1 + 2 * m] // 2
            cols = pl.ds(pl.multiple_of(chip * HD, HD), HD)
            theirs[:, cols] = src[rows:, :]
            out[:, cols] = src[...]


def line_up(place, left, right):
    rows = left[0].shape[0]
    cols = len(left) * HD
    vmem = pl.BlockSpec(memory_space=pltpu.VMEM)
    return pl.pallas_call(
        line_up_kernel,
        out_shape=[jax.ShapeDtypeStruct((r, cols), left[0].dtype) for r in (rows, rows, rows // 2, rows // 2)],
        in_specs=[pl.BlockSpec(memory_space=pltpu.SMEM)] + [vmem] * (2 * len(left)),
        out_specs=[vmem] * 4,
        compiler_params=pltpu.CompilerParams(vmem_limit_bytes=12 * MIB),
        name="line_up",
    )(place, *left, *right)


def add_up_kernel(left, left_last, right, right_last, out):
    rows, half = out.shape[0], out.shape[1] // 2
    for which, (a, b) in enumerate(((left, left_last), (right, right_last))):
        total = a[rows:, :].astype(jnp.float32) + b[rows:, :].astype(jnp.float32)
        out[:, which * half : (which + 1) * half] = total.astype(out.dtype)


def add_up(*shares):
    rows, half = shares[0].shape
    vmem = pl.BlockSpec(memory_space=pltpu.VMEM)
    return pl.pallas_call(
        add_up_kernel,
        out_shape=jax.ShapeDtypeStruct((rows // 2, 2 * half), shares[0].dtype),
        in_specs=[vmem] * 4,
        out_specs=vmem,
        compiler_params=pltpu.CompilerParams(vmem_limit_bytes=12 * MIB),
        name="add_up",
    )(*shares)


def finish_kernel(place, left, left_last, right, right_last, cross, grad_wq, grad_wk, grad_wv):
    core = lax.rem(place[0], 2)
    rows, half = grad_wk.shape

    def add(a, b, cols):
        return (a[:rows, cols].astype(jnp.float32) + b[:rows, cols].astype(jnp.float32)).astype(jnp.bfloat16)

    for h in range(half // HD):
        cols = slice(h * HD, (h + 1) * HD)
        mine, other = add(left, left_last, cols), cross[:, cols]
        grad_wq[:, 2 * h * HD : (2 * h + 1) * HD] = jnp.where(core == 0, mine, other)
        grad_wq[:, (2 * h + 1) * HD : (2 * h + 2) * HD] = jnp.where(core == 0, other, mine)
        mine, other = add(right, right_last, cols), cross[:, half + h * HD : half + (h + 1) * HD]
        grad_wk[:, cols] = jnp.where(core == 0, mine, other)
        grad_wv[:, cols] = jnp.where(core == 0, other, mine)


def finish(place, left, left_last, right, right_last, cross):
    rows, half = cross.shape[0], left.shape[1]
    vmem = pl.BlockSpec(memory_space=pltpu.VMEM)
    return pl.pallas_call(
        finish_kernel,
        out_shape=[jax.ShapeDtypeStruct((rows, w), jnp.bfloat16) for w in (2 * half, half, half)],
        in_specs=[pl.BlockSpec(memory_space=pltpu.SMEM)] + [vmem] * 5,
        out_specs=[vmem] * 3,
        compiler_params=pltpu.CompilerParams(vmem_limit_bytes=14 * MIB),
        name="finish",
    )(place, left, left_last, right, right_last, cross)


def swap(value, axis, by):
    size = lax.axis_size(axis)
    return lax.ppermute(value, axis, [(i, i ^ by) for i in range(size)])


def middle_swap(value):
    levels = lax.axis_size("head")
    pairs = []
    for s in range(lax.axis_size("seq")):
        for h in range(levels):
            to = s * levels + (3 - h) if h in (1, 2) else (s ^ 1) * levels + h
            pairs.append((s * levels + h, to))
    return lax.ppermute(value, ("seq", "head"), pairs)


def wide(value):
    return value.astype(jnp.float32)


def turn_kernel(place, own, peer, out):
    core = lax.rem(place[0], 2)
    rows = own.shape[0]
    strip = out.shape[0] // 2
    for which, src in ((0, own), (1, peer)):
        cols = slice(which * rows, (which + 1) * rows)
        turned = src[...].T

        @pl.when(core == 0)
        def _():
            out[:, cols] = turned

        @pl.when(core == 1)
        def _():
            out[:strip, cols] = turned[strip:]
            out[strip:, cols] = turned[:strip]


def turn(place, own, peer, m, strip):
    rows = own.shape[0]
    spec = pl.BlockSpec((rows, strip), lambda i, place: (0, place[1 + 2 * m] // 2))
    return pl.pallas_call(
        turn_kernel,
        out_shape=jax.ShapeDtypeStruct((strip, 2 * rows), own.dtype),
        grid_spec=pltpu.PrefetchScalarGridSpec(
            num_scalar_prefetch=1,
            grid=(1,),
            in_specs=[spec, spec],
            out_specs=pl.BlockSpec((strip, 2 * rows), lambda i, place: (0, 0)),
        ),
        compiler_params=pltpu.CompilerParams(vmem_limit_bytes=16 * MIB),
        name="turn",
    )(place, own, peer)


def stand_up_queries_kernel(place, mine, other, out):
    core = lax.rem(place[0], 2)
    for h in range(mine.shape[1] // HD):
        cols = slice(h * HD, (h + 1) * HD)
        out[pl.ds(pl.multiple_of((2 * h + core) * HD, HD), HD), :] = mine[:, cols].T
        out[pl.ds(pl.multiple_of((2 * h + 1 - core) * HD, HD), HD), :] = other[:, cols].T


def stand_up_key_values_kernel(place, mine, other, out):
    core = lax.rem(place[0], 2)
    half = mine.shape[1]
    out[pl.ds(pl.multiple_of(core * half, HD), half), :] = mine[...].T
    out[pl.ds(pl.multiple_of((1 - core) * half, HD), half), :] = other[...].T


def stand_up(kernel, place, lined, other):
    rows, cols = other.shape
    spec = pl.BlockSpec((rows, cols), lambda i: (0, 0))
    return pl.pallas_call(
        kernel,
        out_shape=jax.ShapeDtypeStruct((2 * cols, rows), other.dtype),
        grid=(1,),
        in_specs=[pl.BlockSpec(memory_space=pltpu.SMEM), spec, spec],
        out_specs=pl.BlockSpec((2 * cols, rows), lambda i: (0, 0)),
        compiler_params=pltpu.CompilerParams(vmem_limit_bytes=8 * MIB),
        name="stand_up",
    )(place, lined, other)


def share_kernel(order, xq, xkv, w_query, w_key, w_value, out):
    kv_cols = w_key.shape[1]
    total = dot(w_query[...], xq[...], NN)
    total += dot(w_key[...], xkv[:kv_cols, :], NN)
    total += dot(w_value[...], xkv[kv_cols:, :], NN)
    out[...] = total.astype(out.dtype)


def share(order, i, xq, xkv, w_query, w_key, w_value, width):
    rows = xq.shape[1]
    steps = width // SHARE_COLS
    weights = (w_query, w_key, w_value)
    depth = sum(w.shape[1] for w in weights)
    return pl.pallas_call(
        share_kernel,
        out_shape=jax.ShapeDtypeStruct((width, rows), xq.dtype),
        grid_spec=pltpu.PrefetchScalarGridSpec(
            num_scalar_prefetch=1,
            grid=(steps,),
            in_specs=[pl.BlockSpec(x.shape, lambda j, order: (0, 0)) for x in (xq, xkv)]
            + [pl.BlockSpec((SHARE_COLS, w.shape[1]), lambda j, order: (order[i] * steps + j, 0)) for w in weights],
            out_specs=pl.BlockSpec((SHARE_COLS, rows), lambda j, order: (j, 0)),
        ),
        compiler_params=pltpu.CompilerParams(vmem_limit_bytes=14 * MIB),
        cost_estimate=pl.CostEstimate(flops=2 * rows * depth * width, bytes_accessed=2 * depth * width, transcendentals=0),
        name="share",
    )(order, xq, xkv, *weights)


def lay_down_kernel(a, b, c, out):
    total = a[...].astype(jnp.float32) + b[...].astype(jnp.float32) + c[...].astype(jnp.float32)
    out[...] = total.astype(out.dtype).T


def lay_down(a, b, c):
    vmem = pl.BlockSpec(memory_space=pltpu.VMEM)
    return pl.pallas_call(
        lay_down_kernel,
        out_shape=jax.ShapeDtypeStruct(a.shape[::-1], a.dtype),
        in_specs=[vmem] * 3,
        out_specs=vmem,
        compiler_params=pltpu.CompilerParams(vmem_limit_bytes=16 * MIB),
        name="lay_down",
    )(a, b, c)


BLOCK_ORDER = ((3, 2, 1, 0), (0, 3, 2, 1), (3, 0, 1, 2), (0, 1, 2, 3))


def block_body(queries, keys, values, out_grad, normed, w_query, w_key, w_value, valid_len):
    bf = jnp.bfloat16
    seq_size = lax.axis_size("seq")
    rows = queries.shape[0]
    score_scale = (D // H) ** (-0.5)
    me = lax.axis_index("seq")
    core = me % 2
    chip = me // 2
    level = lax.axis_index("head")
    chips = seq_size // 2
    place = jnp.stack([me] + [me ^ m for m in range(seq_size)]).astype(jnp.int32)

    order = jnp.array(BLOCK_ORDER, jnp.int32)[level]
    place, order = lax.optimization_barrier((place, order))
    qg, kv = pack(queries, keys, values, out_grad, seq_size)
    kv = lax.all_to_all(kv, "seq", 0, 0, tiled=True)
    kv_peer = swap(kv, "seq", 1)
    normed_peer = swap(normed, "seq", 1)
    qg, kv, normed, normed_peer = lax.optimization_barrier((qg, kv, normed, normed_peer))
    qg = lax.all_to_all(qg, "seq", 0, 0, tiled=True)
    width = normed.shape[1]
    own_rows = width // seq_size
    strips = [turn(place, normed, normed_peer, m, 2 * own_rows) for m in range(3)]
    strips, qg = lax.optimization_barrier((strips, qg))

    dq, keep, give = attention(place, valid_len, qg, kv, kv_peer, tables(rows, seq_size), score_scale)
    dkv = (keep + wide(swap(give, "seq", 1))).astype(bf)
    dq_parts = [dq[2 * rows * m : 2 * rows * (m + 1)] for m in range(chips)]
    dkv_parts = [dkv[2 * rows * m : 2 * rows * (m + 1)] for m in range(chips)]
    dq_parts = [dq_parts[0]] + [swap(dq_parts[m], "seq", 2 * m) for m in range(1, chips)]
    dkv_parts = [dkv_parts[0]] + [swap(dkv_parts[m], "seq", 2 * m) for m in range(1, chips)]
    normed, normed_peer, dq_parts[1] = lax.optimization_barrier((normed, normed_peer, dq_parts[1]))
    strips = [*strips, turn(place, normed, normed_peer, 3, 2 * own_rows)]
    strips, dq_parts, dkv_parts = lax.optimization_barrier((strips, dq_parts, dkv_parts))
    block_width = width // lax.axis_size("head")

    def left_of(m, lined):
        return jnp.dot(strips[m], lined, preferred_element_type=jnp.float32).astype(bf)

    lined_q, lined_kv, theirs_q, theirs_kv = line_up(place, dq_parts, dkv_parts)
    other_q, other_kv = swap(theirs_q, "seq", 1), swap(theirs_kv, "seq", 1)
    left3_out, right3_out = left_of(3, lined_q), left_of(3, lined_kv)
    left3, right3 = swap(left3_out, "seq", 2), swap(right3_out, "seq", 4)
    left3_out, right3_out, other_q, other_kv = lax.optimization_barrier((left3_out, right3_out, other_q, other_kv))
    xq = stand_up(stand_up_queries_kernel, place, lined_q, other_q)
    xkv = stand_up(stand_up_key_values_kernel, place, lined_kv, other_kv)
    first_out = share(order, 0, xq, xkv, w_query, w_key, w_value, block_width)
    first_in = swap(first_out, "head", 1)
    lined_q, lined_kv, xq, first_out = lax.optimization_barrier((lined_q, lined_kv, xq, first_out))
    left1_out, right2_out = left_of(1, lined_q), left_of(2, lined_kv)
    second_out = share(order, 1, xq, xkv, w_query, w_key, w_value, block_width)
    left3, right3, left1_out, right2_out, second_out, lined_q, lined_kv, xq = lax.optimization_barrier(
        (left3, right3, left1_out, right2_out, second_out, lined_q, lined_kv, xq)
    )
    left1, right2 = swap(left1_out, "seq", 2), swap(right2_out, "seq", 4)
    first_in, left1_out, right2_out, second_out, xq, lined_q, lined_kv = lax.optimization_barrier(
        (first_in, left1_out, right2_out, second_out, xq, lined_q, lined_kv)
    )
    second_in = swap(second_out, "head", 1)
    first_mid = middle_swap((wide(second_out) + wide(first_in)).astype(bf))
    left_out = (wide(left_of(2, lined_q)) + wide(left3)).astype(bf)
    right_out = (wide(left_of(1, lined_kv)) + wide(right3)).astype(bf)
    third = share(order, 2, xq, xkv, w_query, w_key, w_value, block_width)
    left1, right2, left_out, right_out, lined_q, lined_kv, xq = lax.optimization_barrier(
        (left1, right2, left_out, right_out, lined_q, lined_kv, xq)
    )
    left_last, right_last = swap(left_out, "seq", 4), swap(right_out, "seq", 2)
    second_in, first_mid, third, left_out, right_out, lined_q, lined_kv, xq = lax.optimization_barrier(
        (second_in, first_mid, third, left_out, right_out, lined_q, lined_kv, xq)
    )
    inner = (level == 1) | (level == 2)
    third_in = swap(jnp.where(inner, first_mid, third), "head", 1)
    second_mid = middle_swap((wide(third) + wide(second_in)).astype(bf))
    left_sum = (wide(left_of(0, lined_q)) + wide(left1)).astype(bf)
    right_sum = (wide(left_of(0, lined_kv)) + wide(right2)).astype(bf)
    cross = swap(add_up(left_sum, left_last, right_sum, right_last), "seq", 1)
    fourth = share(order, 3, xq, xkv, w_query, w_key, w_value, block_width)
    grad_x = lay_down(fourth, third_in, jnp.where(inner, second_mid, first_in))
    grad_wq, grad_wk, grad_wv = finish(place, left_sum, left_last, right_sum, right_last, cross)
    return (grad_x, grad_wq, grad_wk, grad_wv)


def solution(mesh):
    square = mesh.shape["seq"] == 8 and mesh.shape["head"] == 4
    body = block_body if square else general_body
    placed = (
        P("seq", "head"),
        P("seq", "head"),
        P("seq", "head"),
        P("seq", "head"),
        P("seq", None),
        P(None, "head"),
        P(None, "head"),
        P(None, "head"),
        P(),
    )
    return jax.shard_map(
        body,
        mesh=mesh,
        in_specs=placed,
        out_specs=(P("seq", "head"), P("seq", "head"), P("seq", "head"), P("seq", "head")),
        check_vma=False,
    )
```

profile of v0, /device:TPU:0, one launch (start us, length us, event | category | flops | bytes accessed | tf_op | source)
XLA Modules:
  0.0 220.5 jit_solution(12222642187249471302)
XLA Ops:
  1.1 3.9 %pack.1 = (bf16[8,512,256]{2,1,0:T(8,128)(2,1)}, bf16[8,512,128]{2,1,0:T(8,128)(2,1)}) custom-call(bf16[512,1024]{1,0:T(8,128)(2,1)} %q.1, bf16[512,512]{1,0:T(8,128)(2,1)} %k.1, bf16[512,512]{1,0:T(8,128)(2,1)} %v.1, bf16[512,1024]{1,0:T(8,128)(2,1)} %g.1), custom_call_target="tpu_custom_call" | custom-call | tf_op jit(solution)/shard_map/pack/pallas_call | solution.py:419
  5.0 20.5 %all_to_all.10.refs_1_ = bf16[8,512,128]{2,1,0:T(8,128)(2,1)} all-to-all(bf16[8,512,128]{2,1,0:T(8,128)(2,1)} %get-tuple-element.75), channel_id=1, replica_groups=mesh['seq'=8,'head'=4] {'seq'}, dimensions={0} | all-to-all | bytes 2097152 | tf_op jit(solution)/shard_map/all_to_all | solution.py:652
  25.5 3.6 %all-to-all-start.1 = ((bf16[8,512,256]{2,1,0:T(8,128)(2,1)}), bf16[8,512,256]{2,1,0:T(8,128)(2,1)S(1)}, u32[]{:S(2)}, u32[]{:S(2)}) async-start(bf16[8,512,256]{2,1,0:T(8,128)(2,1)} %get-tuple-element.78), calls=%async_computation.1 | async-start | bytes 4194304 | tf_op jit(solution)/shard_map/all_to_all | solution.py:656
  33.9 2.8 %turn.6 = bf16[1152,1024]{1,0:T(8,128)(2,1)S(1)} custom-call(s32[9]{0:T(128)S(1)} %stack.36.place, bf16[512,4608]{1,0:T(8,128)(2,1)S(1)} %copy-done.1, bf16[512,4608]{1,0:T(8,128)(2,1)} %collective-permute-done.peer), custom_call_target="tpu_custom_call" | custom-call | tf_op jit(solution)/shard_map/turn/pallas_call | solution.py:545
  38.1 2.8 %turn.5 = bf16[1152,1024]{1,0:T(8,128)(2,1)S(1)} custom-call(s32[9]{0:T(128)S(1)} %stack.36.place, bf16[512,4608]{1,0:T(8,128)(2,1)S(1)} %copy-done.1, bf16[512,4608]{1,0:T(8,128)(2,1)} %collective-permute-done.peer), custom_call_target="tpu_custom_call" | custom-call | tf_op jit(solution)/shard_map/turn/pallas_call | solution.py:545
  42.4 2.8 %turn.4 = bf16[1152,1024]{1,0:T(8,128)(2,1)S(1)} custom-call(s32[9]{0:T(128)S(1)} %stack.36.place, bf16[512,4608]{1,0:T(8,128)(2,1)S(1)} %copy-done.1, bf16[512,4608]{1,0:T(8,128)(2,1)} %collective-permute-done.peer), custom_call_target="tpu_custom_call" | custom-call | tf_op jit(solution)/shard_map/turn/pallas_call | solution.py:545
  46.6 9.1 %all-to-all-done.1.refs_0_ = bf16[8,512,256]{2,1,0:T(8,128)(2,1)S(1)} async-done(((bf16[8,512,256]{2,1,0:T(8,128)(2,1)}), bf16[8,512,256]{2,1,0:T(8,128)(2,1)S(1)}, u32[]{:S(2)}, u32[]{:S(2)}) %all-to-all-start.1) | async-done | bytes 2097184 | tf_op jit(solution)/shard_map/all_to_all | solution.py:656
  56.9 32.5 %attention.1 = (bf16[4096,128]{1,0:T(8,128)(2,1)S(1)}, f32[4096,128]{1,0:T(8,128)S(1)}, bf16[4096,128]{1,0:T(8,128)(2,1)S(1)}) custom-call(s32[9]{0:T(128)S(1)} %stack.36.place, s32[8]{0:T(128)S(1)} %copy-done.17, bf16[8,512,256]{2,1,0:T(8,128)(2,1)S(1)} %all-to-all-done.1.refs_0_, bf16[8,512,128]{2,1,0:T(8,128)(2,1)S(1)} %copy-done.16, ...), custom_call_target="tpu_custom_call" | custom-call | flops 25769803776 | bytes 8388608 | tf_op jit(solution)/shard_map/attention/pallas_call | solution.py:358
  95.5 8.9 %collective-permute-done.2.refs_1_ = bf16[1024,128]{1,0:T(8,128)(2,1)S(1)} collective-permute-done((bf16[1024,128]{1,0:T(8,128)(2,1)S(1)}, bf16[1024,128]{1,0:T(8,128)(2,1)S(1)}, u32[]{:S(2)}, u32[]{:S(2)}) %collective-permute-start.2) | collective-permute-done | bytes 262176 | tf_op jit(solution)/shard_map/ppermute | solution.py:507
  105.0 3.0 %turn.7 = bf16[1152,1024]{1,0:T(8,128)(2,1)S(1)} custom-call(s32[9]{0:T(128)S(1)} %stack.36.place, bf16[512,4608]{1,0:T(8,128)(2,1)S(1)} %bitcast.31, bf16[512,4608]{1,0:T(8,128)(2,1)} %collective-permute-done.peer), custom_call_target="tpu_custom_call" | custom-call | tf_op jit(solution)/shard_map/turn/pallas_call | solution.py:545
  108.0 3.0 %collective-permute-done.8.refs_7_ = bf16[1024,128]{1,0:T(8,128)(2,1)S(1)} collective-permute-done((bf16[1024,128]{1,0:T(8,128)(2,1)S(1)}, bf16[1024,128]{1,0:T(8,128)(2,1)S(1)}, u32[]{:S(2)}, u32[]{:S(2)}) %collective-permute-start.8) | collective-permute-done | bytes 262176 | tf_op jit(solution)/shard_map/ppermute | solution.py:507
  111.0 4.5 %collective-permute-done.7.refs_6_ = bf16[1024,128]{1,0:T(8,128)(2,1)S(1)} collective-permute-done((bf16[1024,128]{1,0:T(8,128)(2,1)S(1)}, bf16[1024,128]{1,0:T(8,128)(2,1)S(1)}, u32[]{:S(2)}, u32[]{:S(2)}) %collective-permute-start.7) | collective-permute-done | bytes 262176 | tf_op jit(solution)/shard_map/ppermute | solution.py:507
  123.9 3.5 %share.4 = bf16[1152,512]{1,0:T(8,128)(2,1)S(1)} custom-call(s32[4]{0:T(128)S(1)} %dynamic-slice_bitcast_fusion.order, bf16[1024,512]{1,0:T(8,128)(2,1)S(1)} %stand_up.2.xq, bf16[1024,512]{1,0:T(8,128)(2,1)S(1)} %stand_up.3.xkv, bf16[4608,1024]{1,0:T(8,128)(2,1)S(1)} %bitcast.27, bf16[4608,512]{1,0:T(8,128)(2,1)S(1)} %bitcast.33, bf16[4608,512]{1,0:T(8,128)(2,1)S(1)} %bitcast.35), custom_call_target="tpu_custom_call" | custom-call | flops 2415919104 | bytes 4718592 | tf_op jit(solution)/shard_map/share/pallas_call | solution.py:601
  129.3 3.5 %share.5 = bf16[1152,512]{1,0:T(8,128)(2,1)S(1)} custom-call(s32[4]{0:T(128)S(1)} %dynamic-slice_bitcast_fusion.order, bf16[1024,512]{1,0:T(8,128)(2,1)S(1)} %stand_up.2.xq, bf16[1024,512]{1,0:T(8,128)(2,1)S(1)} %stand_up.3.xkv, bf16[4608,1024]{1,0:T(8,128)(2,1)S(1)} %bitcast.27, bf16[4608,512]{1,0:T(8,128)(2,1)S(1)} %bitcast.33, bf16[4608,512]{1,0:T(8,128)(2,1)S(1)} %bitcast.35), custom_call_target="tpu_custom_call" | custom-call | flops 2415919104 | bytes 4718592 | tf_op jit(solution)/shard_map/share/pallas_call | solution.py:601
  132.8 2.4 %convolution_convert_fusion.5 = bf16[1152,512]{1,0:T(8,128)(2,1)} fusion(bf16[1152,1024]{1,0:T(8,128)(2,1)S(1)} %copy-done.10, bf16[1024,512]{1,0:T(8,128)(2,1)S(1)} %get-tuple-element.133.mine), kind=kOutput, calls=%fused_computation.17 | convolution fusion | flops 1208549376 | bytes 4587520 | tf_op jit(solution)/shard_map/dot_general | solution.py:674
  135.3 2.4 %convolution_convert_fusion.4 = bf16[1152,512]{1,0:T(8,128)(2,1)} fusion(bf16[1152,1024]{1,0:T(8,128)(2,1)S(1)} %copy-done.7, bf16[1024,512]{1,0:T(8,128)(2,1)S(1)} %get-tuple-element.135.mine), kind=kOutput, calls=%fused_computation.16 | convolution fusion | flops 1208549376 | bytes 4587520 | tf_op jit(solution)/shard_map/dot_general | solution.py:674
  137.7 8.9 %collective-permute-done.13 = bf16[1152,512]{1,0:T(8,128)(2,1)S(1)} collective-permute-done((bf16[1152,512]{1,0:T(8,128)(2,1)S(1)}, bf16[1152,512]{1,0:T(8,128)(2,1)S(1)}, u32[]{:S(2)}, u32[]{:S(2)}) %collective-permute-start.13) | collective-permute-done | bytes 1179680 | tf_op jit(solution)/shard_map/ppermute | solution.py:507
  146.6 2.4 %collective-permute-done.12 = bf16[1152,512]{1,0:T(8,128)(2,1)S(1)} collective-permute-done((bf16[1152,512]{1,0:T(8,128)(2,1)S(1)}, bf16[1152,512]{1,0:T(8,128)(2,1)S(1)}, u32[]{:S(2)}, u32[]{:S(2)}) %collective-permute-start.12) | collective-permute-done | bytes 1179680 | tf_op jit(solution)/shard_map/ppermute | solution.py:507
  150.9 4.4 %collective-permute-done.11 = bf16[1152,512]{1,0:T(8,128)(2,1)S(1)} collective-permute-done((bf16[1152,512]{1,0:T(8,128)(2,1)S(1)}, bf16[1152,512]{1,0:T(8,128)(2,1)S(1)}, u32[]{:S(2)}, u32[]{:S(2)}) %collective-permute-start.11) | collective-permute-done | bytes 1179680 | tf_op jit(solution)/shard_map/ppermute | solution.py:507
  156.7 3.3 %collective-permute-start.14 = (bf16[1152,512]{1,0:T(8,128)(2,1)S(1)}, bf16[1152,512]{1,0:T(8,128)(2,1)}, u32[]{:S(2)}, u32[]{:S(2)}) collective-permute-start(bf16[1152,512]{1,0:T(8,128)(2,1)S(1)} %share.5), channel_id=1, source_target_pairs={{0,1},{1,0},{2,3},{3,2},{4,5},{5,4},{6,7},{7,6},{8,9},{9,8},{10,11... | collective-permute-start | bytes 3538952 | tf_op jit(solution)/shard_map/ppermute | solution.py:507
  160.0 3.7 %copy-done = bf16[4608,1024]{1,0:T(8,128)(2,1)S(1)} copy-done((bf16[4608,1024]{1,0:T(8,128)(2,1)S(1)}, bf16[4608,1024]{1,0:T(8,128)(2,1)}, u32[]{:S(2)}) %copy-start) | copy-done | bytes 9437208
  163.6 2.3 %copy-done.2 = bf16[4608,512]{1,0:T(8,128)(2,1)S(1)} copy-done((bf16[4608,512]{1,0:T(8,128)(2,1)S(1)}, bf16[4608,512]{1,0:T(8,128)(2,1)}, u32[]{:S(2)}) %copy-start.2) | copy-done | bytes 4718616
  166.0 2.3 %copy-done.3 = bf16[4608,512]{1,0:T(8,128)(2,1)S(1)} copy-done((bf16[4608,512]{1,0:T(8,128)(2,1)S(1)}, bf16[4608,512]{1,0:T(8,128)(2,1)}, u32[]{:S(2)}) %copy-start.3) | copy-done | bytes 4718616
  168.3 3.5 %share.6 = bf16[1152,512]{1,0:T(8,128)(2,1)S(1)} custom-call(s32[4]{0:T(128)S(1)} %dynamic-slice_bitcast_fusion.order, bf16[1024,512]{1,0:T(8,128)(2,1)S(1)} %stand_up.2.xq, bf16[1024,512]{1,0:T(8,128)(2,1)S(1)} %stand_up.3.xkv, bf16[4608,1024]{1,0:T(8,128)(2,1)S(1)} %copy-done, bf16[4608,512]{1,0:T(8,128)(2,1)S(1)} %copy-done.2, bf16[4608,512]{1,0:T(8,128)(2,1)S(1)} %copy-done.3), custom_call_target="tpu_custom_call" | custom-call | flops 2415919104 | bytes 4718592 | tf_op jit(solution)/shard_map/share/pallas_call | solution.py:601
  178.6 6.5 %collective-permute-done.14 = bf16[1152,512]{1,0:T(8,128)(2,1)} collective-permute-done((bf16[1152,512]{1,0:T(8,128)(2,1)S(1)}, bf16[1152,512]{1,0:T(8,128)(2,1)}, u32[]{:S(2)}, u32[]{:S(2)}) %collective-permute-start.14) | collective-permute-done | bytes 1179680 | tf_op jit(solution)/shard_map/ppermute | solution.py:507
  187.0 4.4 %collective-permute-start.18 = (bf16[1152,512]{1,0:T(8,128)(2,1)S(1)}, bf16[1152,512]{1,0:T(8,128)(2,1)S(1)}, u32[]{:S(2)}, u32[]{:S(2)}) collective-permute-start(bf16[1152,512]{1,0:T(8,128)(2,1)S(1)} %broadcast_select_fusion.1), channel_id=1, source_target_pairs={{0,1},{1,0},{2,3},{3,2},{4,5},{5,4},{6,7},{7,6},{8,9},{9,8},{10,11... | collective-permute-start | bytes 3538952 | tf_op jit(solution)/shard_map/ppermute | solution.py:507
  191.5 2.8 %fusion.2.right = bf16[1152,512]{1,0:T(8,128)(2,1)S(1)} fusion(bf16[1152,1024]{1,0:T(8,128)(2,1)S(1)} %copy-done.5, bf16[1024,512]{1,0:T(8,128)(2,1)S(1)} %copy-done.15, bf16[1152,512]{1,0:T(8,128)(2,1)} %collective-permute-done.17), kind=kOutput, calls=%fused_computation.3 | convolution fusion | flops 1210908672 | bytes 5767168 | tf_op jit(solution)/shard_map/dot_general | solution.py:674
  194.3 2.8 %fusion.5.left = bf16[1152,512]{1,0:T(8,128)(2,1)S(1)} fusion(bf16[1152,1024]{1,0:T(8,128)(2,1)S(1)} %copy-done.5, bf16[1024,512]{1,0:T(8,128)(2,1)S(1)} %copy-done.13, bf16[1152,512]{1,0:T(8,128)(2,1)} %collective-permute-done.16), kind=kOutput, calls=%fused_computation.7 | convolution fusion | flops 1210908672 | bytes 5767168 | tf_op jit(solution)/shard_map/dot_general | solution.py:674
  197.1 5.0 %collective-permute-done.20.left_last = bf16[1152,512]{1,0:T(8,128)(2,1)S(1)} collective-permute-done((bf16[1152,512]{1,0:T(8,128)(2,1)S(1)}, bf16[1152,512]{1,0:T(8,128)(2,1)S(1)}, u32[]{:S(2)}, u32[]{:S(2)}) %collective-permute-start.20) | collective-permute-done | bytes 1179680 | tf_op jit(solution)/shard_map/ppermute | solution.py:507
  203.5 3.5 %share.7.a = bf16[1152,512]{1,0:T(8,128)(2,1)S(1)} custom-call(s32[4]{0:T(128)S(1)} %dynamic-slice_bitcast_fusion.order, bf16[1024,512]{1,0:T(8,128)(2,1)S(1)} %stand_up.2.xq, bf16[1024,512]{1,0:T(8,128)(2,1)S(1)} %stand_up.3.xkv, bf16[4608,1024]{1,0:T(8,128)(2,1)S(1)} %bitcast.29, bf16[4608,512]{1,0:T(8,128)(2,1)S(1)} %copy-done.2, ...), custom_call_target="tpu_custom_call" | custom-call | flops 2415919104 | bytes 4718592 | tf_op jit(solution)/shard_map/share/pallas_call | solution.py:601
  207.2 9.1 %collective-permute-done.18.b = bf16[1152,512]{1,0:T(8,128)(2,1)S(1)} collective-permute-done((bf16[1152,512]{1,0:T(8,128)(2,1)S(1)}, bf16[1152,512]{1,0:T(8,128)(2,1)S(1)}, u32[]{:S(2)}, u32[]{:S(2)}) %collective-permute-start.18) | collective-permute-done | bytes 1179680 | tf_op jit(solution)/shard_map/ppermute | solution.py:507
  217.9 2.7 %finish.1 = (bf16[576,1024]{1,0:T(8,128)(2,1)}, bf16[576,512]{1,0:T(8,128)(2,1)}, bf16[576,512]{1,0:T(8,128)(2,1)}) custom-call(s32[9]{0:T(128)S(1)} %stack.36.place, bf16[1152,512]{1,0:T(8,128)(2,1)S(1)} %fusion.5.left, bf16[1152,512]{1,0:T(8,128)(2,1)S(1)} %collective-permute-done.20.left_last, bf16[1152,512]{1,0:T(8,128)(2,1)S(1)} %fusion.2.right, ...), custom_call_target="tpu_custom_call" | custom-call | tf_op jit(solution)/shard_map/finish/pallas_call | solution.py:495
  (132 shorter events, 42.5 us)
Async XLA Ops:
  0.6 24.9 %collective-permute-start = (bf16[512,4608]{1,0:T(8,128)(2,1)}, bf16[512,4608]{1,0:T(8,128)(2,1)}, u32[]{:S(2)}, u32[]{:S(2)}) collective-permute-start(bf16[512,4608]{1,0:T(8,128)(2,1)} %own.3), channel_id=1, source_target_pairs={{0,4},{4,0},{8,12},{12,8},{16,20},{20,16},{24,28},{28,24},{1,5},{5... | collective-permute-start | bytes 14155784 | tf_op jit(solution)/shard_map/ppermute | solution.py:507
  25.5 30.2 %all-to-all-start.1 = ((bf16[8,512,256]{2,1,0:T(8,128)(2,1)}), bf16[8,512,256]{2,1,0:T(8,128)(2,1)S(1)}, u32[]{:S(2)}, u32[]{:S(2)}) async-start(bf16[8,512,256]{2,1,0:T(8,128)(2,1)} %get-tuple-element.78), calls=%async_computation.1 | async-start | bytes 4194304 | tf_op jit(solution)/shard_map/all_to_all | solution.py:656
  29.1 26.6 %collective-permute-start.1 = (bf16[8,512,128]{2,1,0:T(8,128)(2,1)}, bf16[8,512,128]{2,1,0:T(8,128)(2,1)}, u32[]{:S(2)}, u32[]{:S(2)}) collective-permute-start(bf16[8,512,128]{2,1,0:T(8,128)(2,1)} %all_to_all.10.refs_1_), channel_id=1, source_target_pairs={{0,4},{4,0},{8,12},{12,8},{16,20},{20,16},{24,28},{28,24},{1,5},{5... | collective-permute-start | bytes 3145736 | tf_op jit(solution)/shard_map/ppermute | solution.py:507
  42.4 13.4 %copy-start.17 = (s32[8]{0:T(128)S(1)}, s32[8]{0:T(128)}, u32[]{:S(2)}) copy-start(s32[8]{0:T(128)} %lens.1) | copy-start | bytes 100
  42.4 62.6 %slice-start.6 = ((s8[4718592]{0:T(1024)(128)(4,1)}), s8[524288]{0:T(1024)(128)(4,1)S(1)}, s32[]{:S(2)}) async-start(s8[4718592]{0:T(1024)(128)(4,1)} %bitcast.30), calls=%async_computation.8 | async-start | bytes 1048576
  56.9 48.0 %slice-start.7 = ((s8[4718592]{0:T(1024)(128)(4,1)}), s8[4194304]{0:T(1024)(128)(4,1)S(1)}, s32[]{:S(2)}) async-start(s8[4718592]{0:T(1024)(128)(4,1)} %bitcast.30), calls=%async_computation.9 | async-start | bytes 8388608
  89.4 3.7 %collective-permute-start.5 = (bf16[4096,128]{1,0:T(8,128)(2,1)S(1)}, bf16[4096,128]{1,0:T(8,128)(2,1)S(1)}, u32[]{:S(2)}, u32[]{:S(2)}) collective-permute-start(bf16[4096,128]{1,0:T(8,128)(2,1)S(1)} %get-tuple-element.89), channel_id=1, source_target_pairs={{0,4},{4,0},{8,12},{12,8},{16,20},{20,16},{24,28},{28,24},{1,5},{5... | collective-permute-start | bytes 3145736 | tf_op jit(solution)/shard_map/ppermute | solution.py:507
  89.6 18.4 %collective-permute-start.4 = (bf16[1024,128]{1,0:T(8,128)(2,1)S(1)}, bf16[1024,128]{1,0:T(8,128)(2,1)S(1)}, u32[]{:S(2)}, u32[]{:S(2)}) collective-permute-start(bf16[1024,128]{1,0:T(8,128)(2,1)S(1)} %get-tuple-element.144), channel_id=1, source_target_pairs={{0,24},{4,28},{8,16},{12,20},{16,8},{20,12},{24,0},{28,4},{1,25},{... | collective-permute-start | bytes 786440 | tf_op jit(solution)/shard_map/ppermute | solution.py:507
  90.2 17.8 %collective-permute-start.3 = (bf16[1024,128]{1,0:T(8,128)(2,1)S(1)}, bf16[1024,128]{1,0:T(8,128)(2,1)S(1)}, u32[]{:S(2)}, u32[]{:S(2)}) collective-permute-start(bf16[1024,128]{1,0:T(8,128)(2,1)S(1)} %get-tuple-element.145), channel_id=1, source_target_pairs={{0,16},{4,20},{8,24},{12,28},{16,0},{20,4},{24,8},{28,12},{1,17},{... | collective-permute-start | bytes 786440 | tf_op jit(solution)/shard_map/ppermute | solution.py:507
  91.7 12.7 %collective-permute-start.2 = (bf16[1024,128]{1,0:T(8,128)(2,1)S(1)}, bf16[1024,128]{1,0:T(8,128)(2,1)S(1)}, u32[]{:S(2)}, u32[]{:S(2)}) collective-permute-start(bf16[1024,128]{1,0:T(8,128)(2,1)S(1)} %get-tuple-element.147), channel_id=1, source_target_pairs={{0,8},{4,12},{8,0},{12,4},{16,24},{20,28},{24,16},{28,20},{1,9},{5... | collective-permute-start | bytes 786440 | tf_op jit(solution)/shard_map/ppermute | solution.py:507
  93.4 17.5 %collective-permute-start.8 = (bf16[1024,128]{1,0:T(8,128)(2,1)S(1)}, bf16[1024,128]{1,0:T(8,128)(2,1)S(1)}, u32[]{:S(2)}, u32[]{:S(2)}) collective-permute-start(bf16[1024,128]{1,0:T(8,128)(2,1)S(1)} %get-tuple-element.140), channel_id=1, source_target_pairs={{0,24},{4,28},{8,16},{12,20},{16,8},{20,12},{24,0},{28,4},{1,25},{... | collective-permute-start | bytes 786440 | tf_op jit(solution)/shard_map/ppermute | solution.py:507
  94.1 21.4 %collective-permute-start.7 = (bf16[1024,128]{1,0:T(8,128)(2,1)S(1)}, bf16[1024,128]{1,0:T(8,128)(2,1)S(1)}, u32[]{:S(2)}, u32[]{:S(2)}) collective-permute-start(bf16[1024,128]{1,0:T(8,128)(2,1)S(1)} %get-tuple-element.141), channel_id=1, source_target_pairs={{0,16},{4,20},{8,24},{12,28},{16,0},{20,4},{24,8},{28,12},{1,17},{... | collective-permute-start | bytes 786440 | tf_op jit(solution)/shard_map/ppermute | solution.py:507
  104.4 11.1 %collective-permute-start.6 = (bf16[1024,128]{1,0:T(8,128)(2,1)S(1)}, bf16[1024,128]{1,0:T(8,128)(2,1)S(1)}, u32[]{:S(2)}, u32[]{:S(2)}) collective-permute-start(bf16[1024,128]{1,0:T(8,128)(2,1)S(1)} %get-tuple-element.142), channel_id=1, source_target_pairs={{0,8},{4,12},{8,0},{12,4},{16,24},{20,28},{24,16},{28,20},{1,9},{5... | collective-permute-start | bytes 786440 | tf_op jit(solution)/shard_map/ppermute | solution.py:507
  116.5 16.3 %copy-start.12 = (bf16[1024,512]{1,0:T(8,128)(2,1)}, bf16[1024,512]{1,0:T(8,128)(2,1)S(1)}, u32[]{:S(2)}) copy-start(bf16[1024,512]{1,0:T(8,128)(2,1)S(1)} %get-tuple-element.133.mine) | copy-start | bytes 3145732
  116.5 18.7 %copy-start.14 = (bf16[1024,512]{1,0:T(8,128)(2,1)}, bf16[1024,512]{1,0:T(8,128)(2,1)S(1)}, u32[]{:S(2)}) copy-start(bf16[1024,512]{1,0:T(8,128)(2,1)S(1)} %get-tuple-element.135.mine) | copy-start | bytes 3145732
  116.6 5.3 %collective-permute-start.9 = (bf16[512,512]{1,0:T(8,128)(2,1)S(1)}, bf16[512,512]{1,0:T(8,128)(2,1)S(1)}, u32[]{:S(2)}, u32[]{:S(2)}) collective-permute-start(bf16[512,512]{1,0:T(8,128)(2,1)S(1)} %get-tuple-element.101), channel_id=1, source_target_pairs={{0,4},{4,0},{8,12},{12,8},{16,20},{20,16},{24,28},{28,24},{1,5},{5... | collective-permute-start | bytes 1572872 | tf_op jit(solution)/shard_map/ppermute | solution.py:507
  116.6 5.2 %collective-permute-start.10 = (bf16[512,512]{1,0:T(8,128)(2,1)S(1)}, bf16[512,512]{1,0:T(8,128)(2,1)S(1)}, u32[]{:S(2)}, u32[]{:S(2)}) collective-permute-start(bf16[512,512]{1,0:T(8,128)(2,1)S(1)} %get-tuple-element.102), channel_id=1, source_target_pairs={{0,4},{4,0},{8,12},{12,8},{16,20},{20,16},{24,28},{28,24},{1,5},{5... | collective-permute-start | bytes 1572872 | tf_op jit(solution)/shard_map/ppermute | solution.py:507
  118.5 28.0 %collective-permute-start.13 = (bf16[1152,512]{1,0:T(8,128)(2,1)S(1)}, bf16[1152,512]{1,0:T(8,128)(2,1)S(1)}, u32[]{:S(2)}, u32[]{:S(2)}) collective-permute-start(bf16[1152,512]{1,0:T(8,128)(2,1)S(1)} %convolution_convert_fusion.6), channel_id=1, source_target_pairs={{0,16},{4,20},{8,24},{12,28},{16,0},{20,4},{24,8},{28,12},{1,17},{... | collective-permute-start | bytes 3538952 | tf_op jit(solution)/shard_map/ppermute | solution.py:507
  121.3 27.7 %collective-permute-start.12 = (bf16[1152,512]{1,0:T(8,128)(2,1)S(1)}, bf16[1152,512]{1,0:T(8,128)(2,1)S(1)}, u32[]{:S(2)}, u32[]{:S(2)}) collective-permute-start(bf16[1152,512]{1,0:T(8,128)(2,1)S(1)} %convolution_convert_fusion.7), channel_id=1, source_target_pairs={{0,8},{4,12},{8,0},{12,4},{16,24},{20,28},{24,16},{28,20},{1,9},{5... | collective-permute-start | bytes 3538952 | tf_op jit(solution)/shard_map/ppermute | solution.py:507
  127.5 27.8 %collective-permute-start.11 = (bf16[1152,512]{1,0:T(8,128)(2,1)S(1)}, bf16[1152,512]{1,0:T(8,128)(2,1)S(1)}, u32[]{:S(2)}, u32[]{:S(2)}) collective-permute-start(bf16[1152,512]{1,0:T(8,128)(2,1)S(1)} %share.4), channel_id=1, source_target_pairs={{0,1},{1,0},{2,3},{3,2},{4,5},{5,4},{6,7},{7,6},{8,9},{9,8},{10,11... | collective-permute-start | bytes 3538952 | tf_op jit(solution)/shard_map/ppermute | solution.py:507
  146.5 10.1 %copy-start.20 = (bf16[1152,512]{1,0:T(8,128)(2,1)}, bf16[1152,512]{1,0:T(8,128)(2,1)S(1)}, u32[]{:S(2)}) copy-start(bf16[1152,512]{1,0:T(8,128)(2,1)S(1)} %collective-permute-done.13) | copy-start | bytes 3538948
  149.0 27.1 %collective-permute-start.16 = (bf16[1152,512]{1,0:T(8,128)(2,1)}, bf16[1152,512]{1,0:T(8,128)(2,1)}, u32[]{:S(2)}, u32[]{:S(2)}) collective-permute-start(bf16[1152,512]{1,0:T(8,128)(2,1)} %convolution_convert_fusion.5), channel_id=1, source_target_pairs={{0,8},{4,12},{8,0},{12,4},{16,24},{20,28},{24,16},{28,20},{1,9},{5... | collective-permute-start | bytes 3538952 | tf_op jit(solution)/shard_map/ppermute | solution.py:507
  149.5 26.8 %collective-permute-start.17 = (bf16[1152,512]{1,0:T(8,128)(2,1)}, bf16[1152,512]{1,0:T(8,128)(2,1)}, u32[]{:S(2)}, u32[]{:S(2)}) collective-permute-start(bf16[1152,512]{1,0:T(8,128)(2,1)} %convolution_convert_fusion.4), channel_id=1, source_target_pairs={{0,16},{4,20},{8,24},{12,28},{16,0},{20,4},{24,8},{28,12},{1,17},{... | collective-permute-start | bytes 3538952 | tf_op jit(solution)/shard_map/ppermute | solution.py:507
  156.7 22.0 %collective-permute-start.15 = (bf16[1152,512]{1,0:T(8,128)(2,1)}, bf16[1152,512]{1,0:T(8,128)(2,1)}, u32[]{:S(2)}, u32[]{:S(2)}) collective-permute-start(bf16[1152,512]{1,0:T(8,128)(2,1)} %add_convert_fusion.1), channel_id=1, source_target_pairs={{0,4},{1,2},{2,1},{3,7},{4,0},{5,6},{6,5},{7,3},{8,12},{9,10},{10,... | collective-permute-start | bytes 3538952 | tf_op jit(solution)/shard_map/ppermute | solution.py:517
  156.7 28.5 %collective-permute-start.14 = (bf16[1152,512]{1,0:T(8,128)(2,1)S(1)}, bf16[1152,512]{1,0:T(8,128)(2,1)}, u32[]{:S(2)}, u32[]{:S(2)}) collective-permute-start(bf16[1152,512]{1,0:T(8,128)(2,1)S(1)} %share.5), channel_id=1, source_target_pairs={{0,1},{1,0},{2,3},{3,2},{4,5},{5,4},{6,7},{7,6},{8,9},{9,8},{10,11... | collective-permute-start | bytes 3538952 | tf_op jit(solution)/shard_map/ppermute | solution.py:507
  176.3 25.7 %collective-permute-start.20 = (bf16[1152,512]{1,0:T(8,128)(2,1)S(1)}, bf16[1152,512]{1,0:T(8,128)(2,1)S(1)}, u32[]{:S(2)}, u32[]{:S(2)}) collective-permute-start(bf16[1152,512]{1,0:T(8,128)(2,1)S(1)} %fusion.11), channel_id=1, source_target_pairs={{0,16},{4,20},{8,24},{12,28},{16,0},{20,4},{24,8},{28,12},{1,17},{... | collective-permute-start | bytes 3538952 | tf_op jit(solution)/shard_map/ppermute | solution.py:507
  177.7 25.4 %collective-permute-start.21 = (bf16[1152,512]{1,0:T(8,128)(2,1)S(1)}, bf16[1152,512]{1,0:T(8,128)(2,1)S(1)}, u32[]{:S(2)}, u32[]{:S(2)}) collective-permute-start(bf16[1152,512]{1,0:T(8,128)(2,1)S(1)} %fusion.8), channel_id=1, source_target_pairs={{0,8},{4,12},{8,0},{12,4},{16,24},{20,28},{24,16},{28,20},{1,9},{5... | collective-permute-start | bytes 3538952 | tf_op jit(solution)/shard_map/ppermute | solution.py:507
  186.8 20.3 %collective-permute-start.19 = (bf16[1152,512]{1,0:T(8,128)(2,1)S(1)}, bf16[1152,512]{1,0:T(8,128)(2,1)S(1)}, u32[]{:S(2)}, u32[]{:S(2)}) collective-permute-start(bf16[1152,512]{1,0:T(8,128)(2,1)S(1)} %add_convert_fusion), channel_id=1, source_target_pairs={{0,4},{1,2},{2,1},{3,7},{4,0},{5,6},{6,5},{7,3},{8,12},{9,10},{10,... | collective-permute-start | bytes 3538952 | tf_op jit(solution)/shard_map/ppermute | solution.py:517
  187.0 29.3 %collective-permute-start.18 = (bf16[1152,512]{1,0:T(8,128)(2,1)S(1)}, bf16[1152,512]{1,0:T(8,128)(2,1)S(1)}, u32[]{:S(2)}, u32[]{:S(2)}) collective-permute-start(bf16[1152,512]{1,0:T(8,128)(2,1)S(1)} %broadcast_select_fusion.1), channel_id=1, source_target_pairs={{0,1},{1,0},{2,3},{3,2},{4,5},{5,4},{6,7},{7,6},{8,9},{9,8},{10,11... | collective-permute-start | bytes 3538952 | tf_op jit(solution)/shard_map/ppermute | solution.py:507
  191.5 12.0 %slice-start.3 = ((s8[9437184]{0:T(1024)(128)(4,1)}), s8[4194304]{0:T(1024)(128)(4,1)S(1)}, s32[]{:S(2)}) async-start(s8[9437184]{0:T(1024)(128)(4,1)} %bitcast.28), calls=%async_computation.5 | async-start | bytes 8388608
  191.5 12.0 %slice-start.4 = ((s8[9437184]{0:T(1024)(128)(4,1)}), s8[4194304]{0:T(1024)(128)(4,1)S(1)}, s32[]{:S(2)}) async-start(s8[9437184]{0:T(1024)(128)(4,1)} %bitcast.28), calls=%async_computation.6 | async-start | bytes 8388608
  203.4 14.5 %collective-permute-start.22 = (bf16[576,1024]{1,0:T(8,128)(2,1)S(1)}, bf16[576,1024]{1,0:T(8,128)(2,1)S(1)}, u32[]{:S(2)}, u32[]{:S(2)}) collective-permute-start(bf16[576,1024]{1,0:T(8,128)(2,1)S(1)} %add_up.1), channel_id=1, source_target_pairs={{0,4},{4,0},{8,12},{12,8},{16,20},{20,16},{24,28},{28,24},{1,5},{5... | collective-permute-start | bytes 3538952 | tf_op jit(solution)/shard_map/ppermute | solution.py:507
  (28 other events, 99.5 us)
where the time goes:
time: 218 us; the launch traced here: 221 us
  Pallas kernels  69 us (32%)
  waiting for transfers between devices  63.6 us (29%)
  starting transfers between devices  27.1 us (12%)
  blocking collectives  20.5 us (9%)
  local copies, waits for them, and re-layouts  18.4 us (8%)
  matrix products  16 us (7%)
  other arithmetic  4.7 us (2%)
    ppermute x21, waiting for transfers between devices, swap(): return lax.ppermute(value, axis, [(i, i ^ by) for i in range(size)])  54.5 us
    pallas_call x1, Pallas kernels, attention(): pl.pallas_call(functools.partial(attention_kernel, n, rows, score_scale),...  32.5 us
    ppermute x21, starting transfers between devices, swap(): return lax.ppermute(value, axis, [(i, i ^ by) for i in range(size)])  23.4 us
    all_to_all x1, blocking collectives, block_body(): kv = lax.all_to_all(kv, 'seq', 0, 0, tiled=True)  20.5 us
    unnamed x72, local copies, waits for them, and re-layouts  17.5 us
    dot_general x8, matrix products, left_of(): jnp.dot(strips[m], lined, preferred_element_type=jnp.float32).astype(bf)  16 us
    pallas_call x4, Pallas kernels, share(): pl.pallas_call(share_kernel, out_shape=jax.ShapeDtypeStruct((width, rows)...  14.2 us
    pallas_call x4, Pallas kernels, turn(): pl.pallas_call(turn_kernel, out_shape=jax.ShapeDtypeStruct((strip, 2 * ro...  11.3 us
  transfers between devices with their start and end apart: 24, of which 13 were waited for; matrix products, arithmetic and copies ran while one was open for 10% of the time, Pallas kernels for 15%

commit v1 on v0

--- a/solution.py
+++ b/solution.py
@@ -185,20 +185,22 @@
 
 def attention_kernel(shards, rows, score_scale, place, lens, *refs):
     n = shards
-    qg_in, mine_in, peer_in = refs[:3]
-    cos_r, sin_r, cos_s, sin_s = refs[3:7]
-    dq_out, keep_out, give_out = refs[7:10]
-    (q2, k2, kT, gx, vx, alive, probs, slopes, dps, dq, dk, dv, dqT, qT, gT, sems) = refs[10:]
+    chips = n // 2
+    near, mate = refs[:chips], refs[chips : 2 * chips]
+    refs = refs[2 * chips :]
+    cos_r, sin_r, cos_s, sin_s = refs[:4]
+    dq_out, keep_out, give_out = refs[4:7]
+    (q2, k2, kT, gx, vx, alive, probs, slopes, dps, dq, dk, dv, dqT, qT, gT, sems) = refs[7:]
     me = place[0]
     core = lax.rem(me, 2)
     copies = []
-    mine_at = pl.ds(pl.multiple_of((2 + core) * HD, HD), HD)
-    peer_at = pl.ds(pl.multiple_of((3 - core) * HD, HD), HD)
-    for m in range(n):
-        to = pl.ds(m * rows, rows)
-        copies.append(pltpu.make_async_copy(qg_in.at[m], probs.at[to, pl.ds(0, 2 * HD)], sems.at[0, m]))
-        copies.append(pltpu.make_async_copy(mine_in.at[m], probs.at[to, mine_at], sems.at[1, m]))
-        copies.append(pltpu.make_async_copy(peer_in.at[m], probs.at[to, peer_at], sems.at[2, m]))
+    first_part, second_part, third_part = pl.ds(0, 2 * HD), pl.ds(2 * HD, 2 * HD), pl.ds(4 * HD, 2 * HD)
+    for m in range(chips):
+        own = pl.ds(pl.multiple_of(place[1 + 2 * m] * rows, rows), rows)
+        other = pl.ds(pl.multiple_of(place[2 + 2 * m] * rows, rows), rows)
+        copies.append(pltpu.make_async_copy(near[m].at[:, pl.ds(0, 4 * HD)], probs.at[own, :], sems.at[0, m]))
+        copies.append(pltpu.make_async_copy(mate[m].at[:, second_part], probs.at[other, second_part], sems.at[1, m]))
+        copies.append(pltpu.make_async_copy(mate[m].at[:, third_part], probs.at[other, first_part], sems.at[2, m]))
     for copy in copies:
         copy.start()
     dk[...] = jnp.zeros_like(dk)
@@ -347,8 +349,9 @@
     lax.fori_loop(0, n, unpack, 0)
 
 
-def attention(place, lens, qg, mine, peer, tables, score_scale):
-    n, rows = qg.shape[:2]
+def attention(place, lens, near, mate, tables, score_scale):
+    chips = len(near)
+    n, rows = 2 * chips, near[0].shape[0]
     tokens = n * rows
     room = tokens + KB
     bf, f32 = jnp.bfloat16, jnp.float32
@@ -362,7 +365,7 @@
             jax.ShapeDtypeStruct((tokens, HD), f32),
             jax.ShapeDtypeStruct((tokens, HD), bf),
         ),
-        in_specs=[smem, smem] + [any_spec] * 3 + [vmem] * 4,
+        in_specs=[smem, smem] + [any_spec] * (2 * chips) + [vmem] * 4,
         out_specs=(vmem, vmem, vmem),
         scratch_shapes=[
             pltpu.VMEM((room, 2 * HD), bf),
@@ -380,14 +383,14 @@
             pltpu.VMEM((HD, QB), f32),
             pltpu.VMEM((2 * HD, QB), bf),
             pltpu.VMEM((HD, QB), bf),
-            pltpu.SemaphoreType.DMA((3, n)),
+            pltpu.SemaphoreType.DMA((3, chips)),
         ],
         compiler_params=pltpu.CompilerParams(vmem_limit_bytes=42 * MIB),
         cost_estimate=pl.CostEstimate(
             flops=12 * tokens * tokens * HD, bytes_accessed=16 * tokens * HD, transcendentals=tokens * tokens
         ),
         name="attention",
-    )(place, lens, qg, mine, peer, *tables)
+    )(place, lens, *near, *mate, *tables)
 
 
 def tables(rows, shards):
@@ -399,32 +402,34 @@
     return jnp.cos(within), jnp.sin(within), jnp.cos(start), jnp.sin(start)
 
 
-def pack_kernel(q, k, v, g, qg, kv, sems):
-    n = qg.shape[0]
+def pack_kernel(place, q, k, v, g, *refs):
+    blocks, sems = refs[:-1], refs[-1]
+    core = lax.rem(place[0], 2)
     copies = []
-    for to in range(n):
-        cols, kv_cols = pl.ds(to * HD, HD), pl.ds((to // 2) * HD, HD)
-        copies.append(pltpu.make_async_copy((k, v)[to % 2].at[:, kv_cols], kv.at[to], sems.at[0, to]))
-        copies.append(pltpu.make_async_copy(q.at[:, cols], qg.at[to, :, pl.ds(0, HD)], sems.at[1, to]))
-        copies.append(pltpu.make_async_copy(g.at[:, cols], qg.at[to, :, pl.ds(HD, HD)], sems.at[2, to]))
-    for copy in copies:
-        copy.start()
-    for copy in copies:
-        copy.wait()
-
-
-def pack(q, k, v, g, n):
+    for m, block in enumerate(blocks):
+        chip = place[1 + 2 * m] // 2
+        own, other = 2 * chip + core, 2 * chip + 1 - core
+        for at, (src, head) in enumerate(((q, own), (g, own), (k, chip), (v, chip), (q, other), (g, other))):
+            cols = pl.ds(pl.multiple_of(head * HD, HD), HD)
+            copies.append(pltpu.make_async_copy(src.at[:, cols], block.at[:, pl.ds(at * HD, HD)], sems.at[m, at]))
+    for started in copies:
+        started.start()
+    for started in copies:
+        started.wait()
+
+
+def pack(place, q, k, v, g, n):
     rows = q.shape[0]
     vmem = pl.BlockSpec(memory_space=pltpu.VMEM)
     return pl.pallas_call(
         pack_kernel,
-        out_shape=(jax.ShapeDtypeStruct((n, rows, 2 * HD), q.dtype), jax.ShapeDtypeStruct((n, rows, HD), q.dtype)),
-        in_specs=[pl.BlockSpec(memory_space=pltpu.HBM)] * 4,
-        out_specs=(vmem, vmem),
-        scratch_shapes=[pltpu.SemaphoreType.DMA((3, n))],
+        out_shape=[jax.ShapeDtypeStruct((rows, 6 * HD), q.dtype)] * n,
+        in_specs=[pl.BlockSpec(memory_space=pltpu.SMEM)] + [pl.BlockSpec(memory_space=pltpu.HBM)] * 4,
+        out_specs=[vmem] * n,
+        scratch_shapes=[pltpu.SemaphoreType.DMA((n, 6))],
         compiler_params=pltpu.CompilerParams(vmem_limit_bytes=60 * MIB),
         name="pack",
-    )(q, k, v, g)
+    )(place, q, k, v, g)
 
 
 def line_up_kernel(place, *refs):
@@ -648,18 +653,19 @@
 
     order = jnp.array(BLOCK_ORDER, jnp.int32)[level]
     place, order = lax.optimization_barrier((place, order))
-    qg, kv = pack(queries, keys, values, out_grad, seq_size)
-    kv = lax.all_to_all(kv, "seq", 0, 0, tiled=True)
-    kv_peer = swap(kv, "seq", 1)
+    near = list(pack(place, queries, keys, values, out_grad, chips))
     normed_peer = swap(normed, "seq", 1)
-    qg, kv, normed, normed_peer = lax.optimization_barrier((qg, kv, normed, normed_peer))
-    qg = lax.all_to_all(qg, "seq", 0, 0, tiled=True)
+    normed, normed_peer, _ = lax.optimization_barrier((normed, normed_peer, near[0]))
+    near = [near[0]] + [swap(near[m], "seq", 2 * m) for m in range(1, chips)]
     width = normed.shape[1]
     own_rows = width // seq_size
     strips = [turn(place, normed, normed_peer, m, 2 * own_rows) for m in range(3)]
-    strips, qg = lax.optimization_barrier((strips, qg))
-
-    dq, keep, give = attention(place, valid_len, qg, kv, kv_peer, tables(rows, seq_size), score_scale)
+    for m in range(1, chips):
+        strips[m - 1], near[m] = lax.optimization_barrier((strips[m - 1], near[m]))
+    mate = [swap(part, "seq", 1) for part in near]
+    strips, near, mate = lax.optimization_barrier((strips, near, mate))
+
+    dq, keep, give = attention(place, valid_len, near, mate, tables(rows, seq_size), score_scale)
     dkv = (keep + wide(swap(give, "seq", 1))).astype(bf)
     dq_parts = [dq[2 * rows * m : 2 * rows * (m + 1)] for m in range(chips)]
     dkv_parts = [dkv[2 * rows * m : 2 * rows * (m + 1)] for m in range(chips)]

time: 218 us -> 206 us (0.945); the launches traced: 221 us -> 205 us
  blocking collectives: 20.5 us -> 0 us
  waiting for transfers between devices: 63.6 us -> 77 us
  Pallas kernels: 69 us -> 61.6 us
  local copies, waits for them, and re-layouts: 18.4 us -> 16.1 us
    ppermute x21 -> x27, waiting for transfers between devices: 54.5 us -> 77 us  [swap(): return lax.ppermute(value, axis, [(i, i ^ by) for i in range(size)])]
    all_to_all x1 -> x0, blocking collectives: 20.5 us -> none  [block_body(): kv = lax.all_to_all(kv, 'seq', 0, 0, tiled=True)]
    all_to_all x1 -> x0, waiting for transfers between devices: 9.14 us -> none  [block_body(): qg = lax.all_to_all(qg, 'seq', 0, 0, tiled=True)]
    pallas_call x1, Pallas kernels: 32.5 us -> 23.9 us  [attention(): pl.pallas_call(functools.partial(attention_kernel, n, rows, score_scale),...]
    ppermute x21 -> x27, starting transfers between devices: 23.4 us -> 28.5 us  [swap(): return lax.ppermute(value, axis, [(i, i ^ by) for i in range(size)])]
    all_to_all x1 -> x0, starting transfers between devices: 3.6 us -> none  [block_body(): qg = lax.all_to_all(qg, 'seq', 0, 0, tiled=True)]
    unnamed x72, local copies, waits for them, and re-layouts: 17.5 us -> 14.7 us
  transfers between devices with their start and end apart: 24 -> 29, of which waited for: 13 -> 18; matrix products, arithmetic and copies ran while one was open for 10% -> 11% of each run, Pallas kernels for 15% -> 17%
where the time goes in v1:
time: 206 us; the launch traced here: 205 us
  waiting for transfers between devices  77 us (37%)
  Pallas kernels  61.6 us (30%)
  starting transfers between devices  28.6 us (14%)
  local copies, waits for them, and re-layouts  16.1 us (8%)
  matrix products  16 us (8%)
  other arithmetic  4.7 us (2%)
    ppermute x27, waiting for transfers between devices, swap(): return lax.ppermute(value, axis, [(i, i ^ by) for i in range(size)])  77 us
    ppermute x27, starting transfers between devices, swap(): return lax.ppermute(value, axis, [(i, i ^ by) for i in range(size)])  28.5 us
    pallas_call x1, Pallas kernels, attention(): pl.pallas_call(functools.partial(attention_kernel, n, rows, score_scale),...  23.9 us
    dot_general x8, matrix products, left_of(): jnp.dot(strips[m], lined, preferred_element_type=jnp.float32).astype(bf)  16 us
    unnamed x72, local copies, waits for them, and re-layouts  14.7 us
    pallas_call x4, Pallas kernels, share(): pl.pallas_call(share_kernel, out_shape=jax.ShapeDtypeStruct((width, rows)...  14.2 us
    pallas_call x4, Pallas kernels, turn(): pl.pallas_call(turn_kernel, out_shape=jax.ShapeDtypeStruct((strip, 2 * ro...  11.8 us
    pallas_call x1, Pallas kernels, pack(): pl.pallas_call(pack_kernel, out_shape=[jax.ShapeDtypeStruct((rows, 6 * HD...  4.56 us
  transfers between devices with their start and end apart: 29, of which 18 were waited for; matrix products, arithmetic and copies ran while one was open for 11% of the time, Pallas kernels for 17%

profile of v1, /device:TPU:0, one launch (start us, length us, event | category | flops | bytes accessed | tf_op | source)
XLA Modules:
  0.0 205.2 jit_solution(1647941477439756431)
XLA Ops:
  2.5 4.6 %pack.1 = (bf16[512,768]{1,0:T(8,128)(2,1)}, bf16[512,768]{1,0:T(8,128)(2,1)}, bf16[512,768]{1,0:T(8,128)(2,1)}, bf16[512,768]{1,0:T(8,128)(2,1)}) custom-call(s32[9]{0:T(128)} %stack.36.place, bf16[512,1024]{1,0:T(8,128)(2,1)} %q.1, bf16[512,512]{1,0:T(8,128)(2,1)} %k.1, bf16[512,512]{1,0:T(8,128)(2,1)} %v.1, bf16[512,1024]{1,0:T(8,128)(2,1)} %g.1), custom_call_target="tpu_custom_call" | custom-call | tf_op jit(solution)/shard_map/pack/pallas_call | solution.py:424
  7.0 3.5 %collective-permute-start.3 = (bf16[512,768]{1,0:T(8,128)(2,1)}, bf16[512,768]{1,0:T(8,128)(2,1)S(1)}, u32[]{:S(2)}, u32[]{:S(2)}) collective-permute-start(bf16[512,768]{1,0:T(8,128)(2,1)} %get-tuple-element.94), channel_id=1, source_target_pairs={{0,24},{4,28},{8,16},{12,20},{16,8},{20,12},{24,0},{28,4},{1,25},{... | collective-permute-start | bytes 2359304 | tf_op jit(solution)/shard_map/ppermute | solution.py:512
  11.2 2.3 %copy-done.1 = bf16[512,4608]{1,0:T(8,128)(2,1)S(1)} copy-done((bf16[512,4608]{1,0:T(8,128)(2,1)S(1)}, bf16[512,4608]{1,0:T(8,128)(2,1)}, u32[]{:S(2)}) %copy-start.1) | copy-done | bytes 4718616
  13.6 2.8 %turn.6 = bf16[1152,1024]{1,0:T(8,128)(2,1)S(1)} custom-call(s32[9]{0:T(128)S(1)} %copy-done.15, bf16[512,4608]{1,0:T(8,128)(2,1)S(1)} %copy-done.1, bf16[512,4608]{1,0:T(8,128)(2,1)} %collective-permute-done.peer), custom_call_target="tpu_custom_call" | custom-call | tf_op jit(solution)/shard_map/turn/pallas_call | solution.py:550
  16.4 3.0 %turn.5 = bf16[1152,1024]{1,0:T(8,128)(2,1)S(1)} custom-call(s32[9]{0:T(128)S(1)} %copy-done.15, bf16[512,4608]{1,0:T(8,128)(2,1)S(1)} %copy-done.1, bf16[512,4608]{1,0:T(8,128)(2,1)} %collective-permute-done.peer), custom_call_target="tpu_custom_call" | custom-call | tf_op jit(solution)/shard_map/turn/pallas_call | solution.py:550
  20.8 3.1 %turn.4 = bf16[1152,1024]{1,0:T(8,128)(2,1)S(1)} custom-call(s32[9]{0:T(128)S(1)} %copy-done.15, bf16[512,4608]{1,0:T(8,128)(2,1)S(1)} %copy-done.1, bf16[512,4608]{1,0:T(8,128)(2,1)} %collective-permute-done.peer), custom_call_target="tpu_custom_call" | custom-call | tf_op jit(solution)/shard_map/turn/pallas_call | solution.py:550
  25.3 3.9 %collective-permute-done.3.refs_3_ = bf16[512,768]{1,0:T(8,128)(2,1)S(1)} collective-permute-done((bf16[512,768]{1,0:T(8,128)(2,1)}, bf16[512,768]{1,0:T(8,128)(2,1)S(1)}, u32[]{:S(2)}, u32[]{:S(2)}) %collective-permute-start.3) | collective-permute-done | bytes 786464 | tf_op jit(solution)/shard_map/ppermute | solution.py:512
  29.2 16.6 %collective-permute-done.2.refs_2_ = bf16[512,768]{1,0:T(8,128)(2,1)S(1)} collective-permute-done((bf16[512,768]{1,0:T(8,128)(2,1)}, bf16[512,768]{1,0:T(8,128)(2,1)S(1)}, u32[]{:S(2)}, u32[]{:S(2)}) %collective-permute-start.2) | collective-permute-done | bytes 786464 | tf_op jit(solution)/shard_map/ppermute | solution.py:512
  49.2 23.9 %attention.1 = (bf16[4096,128]{1,0:T(8,128)(2,1)S(1)}, f32[4096,128]{1,0:T(8,128)S(1)}, bf16[4096,128]{1,0:T(8,128)(2,1)S(1)}) custom-call(s32[9]{0:T(128)S(1)} %copy-done.15, s32[8]{0:T(128)S(1)} %copy-done.17, bf16[512,768]{1,0:T(8,128)(2,1)S(1)} %copy-done.16, bf16[512,768]{1,0:T(8,128)(2,1)S(1)} %collective-permute-done.1.refs_1_, ...), custom_call_target="tpu_custom_call" | custom-call | flops 25769803776 | bytes 8388608 | tf_op jit(solution)/shard_map/attention/pallas_call | solution.py:361
  80.5 8.9 %collective-permute-done.8.refs_1_ = bf16[1024,128]{1,0:T(8,128)(2,1)S(1)} collective-permute-done((bf16[1024,128]{1,0:T(8,128)(2,1)S(1)}, bf16[1024,128]{1,0:T(8,128)(2,1)S(1)}, u32[]{:S(2)}, u32[]{:S(2)}) %collective-permute-start.8) | collective-permute-done | bytes 262176 | tf_op jit(solution)/shard_map/ppermute | solution.py:512
  90.1 3.0 %turn.7 = bf16[1152,1024]{1,0:T(8,128)(2,1)S(1)} custom-call(s32[9]{0:T(128)S(1)} %copy-done.15, bf16[512,4608]{1,0:T(8,128)(2,1)S(1)} %bitcast.31, bf16[512,4608]{1,0:T(8,128)(2,1)} %collective-permute-done.peer), custom_call_target="tpu_custom_call" | custom-call | tf_op jit(solution)/shard_map/turn/pallas_call | solution.py:550
  94.8 5.0 %collective-permute-done.13.refs_6_ = bf16[1024,128]{1,0:T(8,128)(2,1)S(1)} collective-permute-done((bf16[1024,128]{1,0:T(8,128)(2,1)S(1)}, bf16[1024,128]{1,0:T(8,128)(2,1)S(1)}, u32[]{:S(2)}, u32[]{:S(2)}) %collective-permute-start.13) | collective-permute-done | bytes 262176 | tf_op jit(solution)/shard_map/ppermute | solution.py:512
  108.7 3.5 %share.4 = bf16[1152,512]{1,0:T(8,128)(2,1)S(1)} custom-call(s32[4]{0:T(128)S(1)} %dynamic-slice_bitcast_fusion.order, bf16[1024,512]{1,0:T(8,128)(2,1)S(1)} %stand_up.2.xq, bf16[1024,512]{1,0:T(8,128)(2,1)S(1)} %stand_up.3.xkv, bf16[4608,1024]{1,0:T(8,128)(2,1)S(1)} %bitcast.27, bf16[4608,512]{1,0:T(8,128)(2,1)S(1)} %bitcast.33, bf16[4608,512]{1,0:T(8,128)(2,1)S(1)} %bitcast.35), custom_call_target="tpu_custom_call" | custom-call | flops 2415919104 | bytes 4718592 | tf_op jit(solution)/shard_map/share/pallas_call | solution.py:606
  113.9 3.5 %share.5 = bf16[1152,512]{1,0:T(8,128)(2,1)S(1)} custom-call(s32[4]{0:T(128)S(1)} %dynamic-slice_bitcast_fusion.order, bf16[1024,512]{1,0:T(8,128)(2,1)S(1)} %stand_up.2.xq, bf16[1024,512]{1,0:T(8,128)(2,1)S(1)} %stand_up.3.xkv, bf16[4608,1024]{1,0:T(8,128)(2,1)S(1)} %bitcast.27, bf16[4608,512]{1,0:T(8,128)(2,1)S(1)} %bitcast.33, bf16[4608,512]{1,0:T(8,128)(2,1)S(1)} %bitcast.35), custom_call_target="tpu_custom_call" | custom-call | flops 2415919104 | bytes 4718592 | tf_op jit(solution)/shard_map/share/pallas_call | solution.py:606
  117.5 2.4 %convolution_convert_fusion.5 = bf16[1152,512]{1,0:T(8,128)(2,1)} fusion(bf16[1152,1024]{1,0:T(8,128)(2,1)S(1)} %copy-done.9, bf16[1024,512]{1,0:T(8,128)(2,1)S(1)} %get-tuple-element.159.mine), kind=kOutput, calls=%fused_computation.17 | convolution fusion | flops 1208549376 | bytes 4587520 | tf_op jit(solution)/shard_map/dot_general | solution.py:680
  119.9 2.4 %convolution_convert_fusion.4 = bf16[1152,512]{1,0:T(8,128)(2,1)} fusion(bf16[1152,1024]{1,0:T(8,128)(2,1)S(1)} %turn.6, bf16[1024,512]{1,0:T(8,128)(2,1)S(1)} %get-tuple-element.161.mine), kind=kOutput, calls=%fused_computation.16 | convolution fusion | flops 1208549376 | bytes 4587520 | tf_op jit(solution)/shard_map/dot_general | solution.py:680
  122.3 8.9 %collective-permute-done.19 = bf16[1152,512]{1,0:T(8,128)(2,1)S(1)} collective-permute-done((bf16[1152,512]{1,0:T(8,128)(2,1)S(1)}, bf16[1152,512]{1,0:T(8,128)(2,1)S(1)}, u32[]{:S(2)}, u32[]{:S(2)}) %collective-permute-start.19) | collective-permute-done | bytes 1179680 | tf_op jit(solution)/shard_map/ppermute | solution.py:512
  131.2 2.6 %collective-permute-done.18 = bf16[1152,512]{1,0:T(8,128)(2,1)S(1)} collective-permute-done((bf16[1152,512]{1,0:T(8,128)(2,1)S(1)}, bf16[1152,512]{1,0:T(8,128)(2,1)S(1)}, u32[]{:S(2)}, u32[]{:S(2)}) %collective-permute-start.18) | collective-permute-done | bytes 1179680 | tf_op jit(solution)/shard_map/ppermute | solution.py:512
  135.8 4.2 %collective-permute-done.17 = bf16[1152,512]{1,0:T(8,128)(2,1)S(1)} collective-permute-done((bf16[1152,512]{1,0:T(8,128)(2,1)S(1)}, bf16[1152,512]{1,0:T(8,128)(2,1)S(1)}, u32[]{:S(2)}, u32[]{:S(2)}) %collective-permute-start.17) | collective-permute-done | bytes 1179680 | tf_op jit(solution)/shard_map/ppermute | solution.py:512
  141.4 3.1 %collective-permute-start.20 = (bf16[1152,512]{1,0:T(8,128)(2,1)S(1)}, bf16[1152,512]{1,0:T(8,128)(2,1)}, u32[]{:S(2)}, u32[]{:S(2)}) collective-permute-start(bf16[1152,512]{1,0:T(8,128)(2,1)S(1)} %share.5), channel_id=1, source_target_pairs={{0,1},{1,0},{2,3},{3,2},{4,5},{5,4},{6,7},{7,6},{8,9},{9,8},{10,11... | collective-permute-start | bytes 3538952 | tf_op jit(solution)/shard_map/ppermute | solution.py:512
  144.6 3.7 %copy-done = bf16[4608,1024]{1,0:T(8,128)(2,1)S(1)} copy-done((bf16[4608,1024]{1,0:T(8,128)(2,1)S(1)}, bf16[4608,1024]{1,0:T(8,128)(2,1)}, u32[]{:S(2)}) %copy-start) | copy-done | bytes 9437208
  148.3 2.3 %copy-done.2 = bf16[4608,512]{1,0:T(8,128)(2,1)S(1)} copy-done((bf16[4608,512]{1,0:T(8,128)(2,1)S(1)}, bf16[4608,512]{1,0:T(8,128)(2,1)}, u32[]{:S(2)}) %copy-start.2) | copy-done | bytes 4718616
  150.6 2.3 %copy-done.3 = bf16[4608,512]{1,0:T(8,128)(2,1)S(1)} copy-done((bf16[4608,512]{1,0:T(8,128)(2,1)S(1)}, bf16[4608,512]{1,0:T(8,128)(2,1)}, u32[]{:S(2)}) %copy-start.3) | copy-done | bytes 4718616
  152.9 3.5 %share.6 = bf16[1152,512]{1,0:T(8,128)(2,1)S(1)} custom-call(s32[4]{0:T(128)S(1)} %dynamic-slice_bitcast_fusion.order, bf16[1024,512]{1,0:T(8,128)(2,1)S(1)} %stand_up.2.xq, bf16[1024,512]{1,0:T(8,128)(2,1)S(1)} %stand_up.3.xkv, bf16[4608,1024]{1,0:T(8,128)(2,1)S(1)} %copy-done, bf16[4608,512]{1,0:T(8,128)(2,1)S(1)} %copy-done.2, bf16[4608,512]{1,0:T(8,128)(2,1)S(1)} %copy-done.3), custom_call_target="tpu_custom_call" | custom-call | flops 2415919104 | bytes 4718592 | tf_op jit(solution)/shard_map/share/pallas_call | solution.py:606
  163.3 6.6 %collective-permute-done.20 = bf16[1152,512]{1,0:T(8,128)(2,1)} collective-permute-done((bf16[1152,512]{1,0:T(8,128)(2,1)S(1)}, bf16[1152,512]{1,0:T(8,128)(2,1)}, u32[]{:S(2)}, u32[]{:S(2)}) %collective-permute-start.20) | collective-permute-done | bytes 1179680 | tf_op jit(solution)/shard_map/ppermute | solution.py:512
  171.8 4.3 %collective-permute-start.24 = (bf16[1152,512]{1,0:T(8,128)(2,1)S(1)}, bf16[1152,512]{1,0:T(8,128)(2,1)S(1)}, u32[]{:S(2)}, u32[]{:S(2)}) collective-permute-start(bf16[1152,512]{1,0:T(8,128)(2,1)S(1)} %broadcast_select_fusion.1), channel_id=1, source_target_pairs={{0,1},{1,0},{2,3},{3,2},{4,5},{5,4},{6,7},{7,6},{8,9},{9,8},{10,11... | collective-permute-start | bytes 3538952 | tf_op jit(solution)/shard_map/ppermute | solution.py:512
  176.1 2.8 %fusion.2.right = bf16[1152,512]{1,0:T(8,128)(2,1)S(1)} fusion(bf16[1152,1024]{1,0:T(8,128)(2,1)S(1)} %copy-done.5, bf16[1024,512]{1,0:T(8,128)(2,1)S(1)} %copy-done.14, bf16[1152,512]{1,0:T(8,128)(2,1)} %collective-permute-done.23), kind=kOutput, calls=%fused_computation.3 | convolution fusion | flops 1210908672 | bytes 5767168 | tf_op jit(solution)/shard_map/dot_general | solution.py:680
  178.9 2.8 %fusion.5.left = bf16[1152,512]{1,0:T(8,128)(2,1)S(1)} fusion(bf16[1152,1024]{1,0:T(8,128)(2,1)S(1)} %copy-done.5, bf16[1024,512]{1,0:T(8,128)(2,1)S(1)} %copy-done.12, bf16[1152,512]{1,0:T(8,128)(2,1)} %collective-permute-done.22), kind=kOutput, calls=%fused_computation.7 | convolution fusion | flops 1210908672 | bytes 5767168 | tf_op jit(solution)/shard_map/dot_general | solution.py:680
  181.7 5.2 %collective-permute-done.26.left_last = bf16[1152,512]{1,0:T(8,128)(2,1)S(1)} collective-permute-done((bf16[1152,512]{1,0:T(8,128)(2,1)S(1)}, bf16[1152,512]{1,0:T(8,128)(2,1)S(1)}, u32[]{:S(2)}, u32[]{:S(2)}) %collective-permute-start.26) | collective-permute-done | bytes 1179680 | tf_op jit(solution)/shard_map/ppermute | solution.py:512
  188.4 3.5 %share.7.a = bf16[1152,512]{1,0:T(8,128)(2,1)S(1)} custom-call(s32[4]{0:T(128)S(1)} %dynamic-slice_bitcast_fusion.order, bf16[1024,512]{1,0:T(8,128)(2,1)S(1)} %stand_up.2.xq, bf16[1024,512]{1,0:T(8,128)(2,1)S(1)} %stand_up.3.xkv, bf16[4608,1024]{1,0:T(8,128)(2,1)S(1)} %bitcast.29, bf16[4608,512]{1,0:T(8,128)(2,1)S(1)} %copy-done.2, ...), custom_call_target="tpu_custom_call" | custom-call | flops 2415919104 | bytes 4718592 | tf_op jit(solution)/shard_map/share/pallas_call | solution.py:606
  192.1 8.9 %collective-permute-done.24.b = bf16[1152,512]{1,0:T(8,128)(2,1)S(1)} collective-permute-done((bf16[1152,512]{1,0:T(8,128)(2,1)S(1)}, bf16[1152,512]{1,0:T(8,128)(2,1)S(1)}, u32[]{:S(2)}, u32[]{:S(2)}) %collective-permute-start.24) | collective-permute-done | bytes 1179680 | tf_op jit(solution)/shard_map/ppermute | solution.py:512
  202.5 2.7 %finish.1 = (bf16[576,1024]{1,0:T(8,128)(2,1)}, bf16[576,512]{1,0:T(8,128)(2,1)}, bf16[576,512]{1,0:T(8,128)(2,1)}) custom-call(s32[9]{0:T(128)S(1)} %copy-done.15, bf16[1152,512]{1,0:T(8,128)(2,1)S(1)} %fusion.5.left, bf16[1152,512]{1,0:T(8,128)(2,1)S(1)} %collective-permute-done.26.left_last, bf16[1152,512]{1,0:T(8,128)(2,1)S(1)} %fusion.2.right, ...), custom_call_target="tpu_custom_call" | custom-call | tf_op jit(solution)/shard_map/finish/pallas_call | solution.py:500
  (141 shorter events, 44.0 us)
Async XLA Ops:
  0.6 10.6 %collective-permute-start = (bf16[512,4608]{1,0:T(8,128)(2,1)}, bf16[512,4608]{1,0:T(8,128)(2,1)}, u32[]{:S(2)}, u32[]{:S(2)}) collective-permute-start(bf16[512,4608]{1,0:T(8,128)(2,1)} %own.3), channel_id=1, source_target_pairs={{0,4},{4,0},{8,12},{12,8},{16,20},{20,16},{24,28},{28,24},{1,5},{5... | collective-permute-start | bytes 14155784 | tf_op jit(solution)/shard_map/ppermute | solution.py:512
  7.0 22.2 %collective-permute-start.3 = (bf16[512,768]{1,0:T(8,128)(2,1)}, bf16[512,768]{1,0:T(8,128)(2,1)S(1)}, u32[]{:S(2)}, u32[]{:S(2)}) collective-permute-start(bf16[512,768]{1,0:T(8,128)(2,1)} %get-tuple-element.94), channel_id=1, source_target_pairs={{0,24},{4,28},{8,16},{12,20},{16,8},{20,12},{24,0},{28,4},{1,25},{... | collective-permute-start | bytes 2359304 | tf_op jit(solution)/shard_map/ppermute | solution.py:512
  10.6 35.3 %collective-permute-start.2 = (bf16[512,768]{1,0:T(8,128)(2,1)}, bf16[512,768]{1,0:T(8,128)(2,1)S(1)}, u32[]{:S(2)}, u32[]{:S(2)}) collective-permute-start(bf16[512,768]{1,0:T(8,128)(2,1)} %get-tuple-element.92), channel_id=1, source_target_pairs={{0,16},{4,20},{8,24},{12,28},{16,0},{20,4},{24,8},{28,12},{1,17},{... | collective-permute-start | bytes 2359304 | tf_op jit(solution)/shard_map/ppermute | solution.py:512
  11.1 35.0 %collective-permute-start.1 = (bf16[512,768]{1,0:T(8,128)(2,1)}, bf16[512,768]{1,0:T(8,128)(2,1)S(1)}, u32[]{:S(2)}, u32[]{:S(2)}) collective-permute-start(bf16[512,768]{1,0:T(8,128)(2,1)} %get-tuple-element.90), channel_id=1, source_target_pairs={{0,8},{4,12},{8,0},{12,4},{16,24},{20,28},{24,16},{28,20},{1,9},{5... | collective-permute-start | bytes 2359304 | tf_op jit(solution)/shard_map/ppermute | solution.py:512
  11.2 36.3 %collective-permute-start.4 = (bf16[512,768]{1,0:T(8,128)(2,1)}, bf16[512,768]{1,0:T(8,128)(2,1)S(1)}, u32[]{:S(2)}, u32[]{:S(2)}) collective-permute-start(bf16[512,768]{1,0:T(8,128)(2,1)} %get-tuple-element.102.refs_0_), channel_id=1, source_target_pairs={{0,4},{4,0},{8,12},{12,8},{16,20},{20,16},{24,28},{28,24},{1,5},{5... | collective-permute-start | bytes 2359304 | tf_op jit(solution)/shard_map/ppermute | solution.py:512
  16.4 103.6 %copy-start.6 = (bf16[1152,1024]{1,0:T(8,128)(2,1)}, bf16[1152,1024]{1,0:T(8,128)(2,1)S(1)}, u32[]{:S(2)}) copy-start(bf16[1152,1024]{1,0:T(8,128)(2,1)S(1)} %turn.6) | copy-start | bytes 7077892
  20.8 69.3 %slice-start.6 = ((s8[4718592]{0:T(1024)(128)(4,1)}), s8[4194304]{0:T(1024)(128)(4,1)S(1)}, s32[]{:S(2)}) async-start(s8[4718592]{0:T(1024)(128)(4,1)} %bitcast.30), calls=%async_computation.6 | async-start | bytes 8388608
  29.2 18.3 %collective-permute-start.7 = (bf16[512,768]{1,0:T(8,128)(2,1)S(1)}, bf16[512,768]{1,0:T(8,128)(2,1)S(1)}, u32[]{:S(2)}, u32[]{:S(2)}) collective-permute-start(bf16[512,768]{1,0:T(8,128)(2,1)S(1)} %collective-permute-done.3.refs_3_), channel_id=1, source_target_pairs={{0,4},{4,0},{8,12},{12,8},{16,20},{20,16},{24,28},{28,24},{1,5},{5... | collective-permute-start | bytes 2359304 | tf_op jit(solution)/shard_map/ppermute | solution.py:512
  45.8 2.3 %collective-permute-start.6 = (bf16[512,768]{1,0:T(8,128)(2,1)S(1)}, bf16[512,768]{1,0:T(8,128)(2,1)S(1)}, u32[]{:S(2)}, u32[]{:S(2)}) collective-permute-start(bf16[512,768]{1,0:T(8,128)(2,1)S(1)} %collective-permute-done.2.refs_2_), channel_id=1, source_target_pairs={{0,4},{4,0},{8,12},{12,8},{16,20},{20,16},{24,28},{28,24},{1,5},{5... | collective-permute-start | bytes 2359304 | tf_op jit(solution)/shard_map/ppermute | solution.py:512
  46.1 3.1 %collective-permute-start.5 = (bf16[512,768]{1,0:T(8,128)(2,1)S(1)}, bf16[512,768]{1,0:T(8,128)(2,1)S(1)}, u32[]{:S(2)}, u32[]{:S(2)}) collective-permute-start(bf16[512,768]{1,0:T(8,128)(2,1)S(1)} %collective-permute-done.1.refs_1_), channel_id=1, source_target_pairs={{0,4},{4,0},{8,12},{12,8},{16,20},{20,16},{24,28},{28,24},{1,5},{5... | collective-permute-start | bytes 2359304 | tf_op jit(solution)/shard_map/ppermute | solution.py:512
  49.2 40.9 %slice-start.7 = ((s8[4718592]{0:T(1024)(128)(4,1)}), s8[524288]{0:T(1024)(128)(4,1)S(1)}, s32[]{:S(2)}) async-start(s8[4718592]{0:T(1024)(128)(4,1)} %bitcast.30), calls=%async_computation.7 | async-start | bytes 1048576
  73.2 3.8 %collective-permute-start.11 = (bf16[4096,128]{1,0:T(8,128)(2,1)S(1)}, bf16[4096,128]{1,0:T(8,128)(2,1)S(1)}, u32[]{:S(2)}, u32[]{:S(2)}) collective-permute-start(bf16[4096,128]{1,0:T(8,128)(2,1)S(1)} %get-tuple-element.115), channel_id=1, source_target_pairs={{0,4},{4,0},{8,12},{12,8},{16,20},{20,16},{24,28},{28,24},{1,5},{5... | collective-permute-start | bytes 3145736 | tf_op jit(solution)/shard_map/ppermute | solution.py:512
  73.4 19.7 %collective-permute-start.10 = (bf16[1024,128]{1,0:T(8,128)(2,1)S(1)}, bf16[1024,128]{1,0:T(8,128)(2,1)S(1)}, u32[]{:S(2)}, u32[]{:S(2)}) collective-permute-start(bf16[1024,128]{1,0:T(8,128)(2,1)S(1)} %get-tuple-element.170), channel_id=1, source_target_pairs={{0,24},{4,28},{8,16},{12,20},{16,8},{20,12},{24,0},{28,4},{1,25},{... | collective-permute-start | bytes 786440 | tf_op jit(solution)/shard_map/ppermute | solution.py:512
  75.3 17.8 %collective-permute-start.9 = (bf16[1024,128]{1,0:T(8,128)(2,1)S(1)}, bf16[1024,128]{1,0:T(8,128)(2,1)S(1)}, u32[]{:S(2)}, u32[]{:S(2)}) collective-permute-start(bf16[1024,128]{1,0:T(8,128)(2,1)S(1)} %get-tuple-element.171), channel_id=1, source_target_pairs={{0,16},{4,20},{8,24},{12,28},{16,0},{20,4},{24,8},{28,12},{1,17},{... | collective-permute-start | bytes 786440 | tf_op jit(solution)/shard_map/ppermute | solution.py:512
  76.6 12.8 %collective-permute-start.8 = (bf16[1024,128]{1,0:T(8,128)(2,1)S(1)}, bf16[1024,128]{1,0:T(8,128)(2,1)S(1)}, u32[]{:S(2)}, u32[]{:S(2)}) collective-permute-start(bf16[1024,128]{1,0:T(8,128)(2,1)S(1)} %get-tuple-element.173), channel_id=1, source_target_pairs={{0,8},{4,12},{8,0},{12,4},{16,24},{20,28},{24,16},{28,20},{1,9},{5... | collective-permute-start | bytes 786440 | tf_op jit(solution)/shard_map/ppermute | solution.py:512
  77.3 17.6 %collective-permute-start.14 = (bf16[1024,128]{1,0:T(8,128)(2,1)S(1)}, bf16[1024,128]{1,0:T(8,128)(2,1)S(1)}, u32[]{:S(2)}, u32[]{:S(2)}) collective-permute-start(bf16[1024,128]{1,0:T(8,128)(2,1)S(1)} %get-tuple-element.166), channel_id=1, source_target_pairs={{0,24},{4,28},{8,16},{12,20},{16,8},{20,12},{24,0},{28,4},{1,25},{... | collective-permute-start | bytes 786440 | tf_op jit(solution)/shard_map/ppermute | solution.py:512
  79.2 20.7 %collective-permute-start.13 = (bf16[1024,128]{1,0:T(8,128)(2,1)S(1)}, bf16[1024,128]{1,0:T(8,128)(2,1)S(1)}, u32[]{:S(2)}, u32[]{:S(2)}) collective-permute-start(bf16[1024,128]{1,0:T(8,128)(2,1)S(1)} %get-tuple-element.167), channel_id=1, source_target_pairs={{0,16},{4,20},{8,24},{12,28},{16,0},{20,4},{24,8},{28,12},{1,17},{... | collective-permute-start | bytes 786440 | tf_op jit(solution)/shard_map/ppermute | solution.py:512
  89.4 10.7 %collective-permute-start.12 = (bf16[1024,128]{1,0:T(8,128)(2,1)S(1)}, bf16[1024,128]{1,0:T(8,128)(2,1)S(1)}, u32[]{:S(2)}, u32[]{:S(2)}) collective-permute-start(bf16[1024,128]{1,0:T(8,128)(2,1)S(1)} %get-tuple-element.168), channel_id=1, source_target_pairs={{0,8},{4,12},{8,0},{12,4},{16,24},{20,28},{24,16},{28,20},{1,9},{5... | collective-permute-start | bytes 786440 | tf_op jit(solution)/shard_map/ppermute | solution.py:512
  101.2 5.5 %collective-permute-start.15 = (bf16[512,512]{1,0:T(8,128)(2,1)S(1)}, bf16[512,512]{1,0:T(8,128)(2,1)S(1)}, u32[]{:S(2)}, u32[]{:S(2)}) collective-permute-start(bf16[512,512]{1,0:T(8,128)(2,1)S(1)} %get-tuple-element.127), channel_id=1, source_target_pairs={{0,4},{4,0},{8,12},{12,8},{16,20},{20,16},{24,28},{28,24},{1,5},{5... | collective-permute-start | bytes 1572872 | tf_op jit(solution)/shard_map/ppermute | solution.py:512
  101.3 5.4 %collective-permute-start.16 = (bf16[512,512]{1,0:T(8,128)(2,1)S(1)}, bf16[512,512]{1,0:T(8,128)(2,1)S(1)}, u32[]{:S(2)}, u32[]{:S(2)}) collective-permute-start(bf16[512,512]{1,0:T(8,128)(2,1)S(1)} %get-tuple-element.128), channel_id=1, source_target_pairs={{0,4},{4,0},{8,12},{12,8},{16,20},{20,16},{24,28},{28,24},{1,5},{5... | collective-permute-start | bytes 1572872 | tf_op jit(solution)/shard_map/ppermute | solution.py:512
  103.2 28.0 %collective-permute-start.19 = (bf16[1152,512]{1,0:T(8,128)(2,1)S(1)}, bf16[1152,512]{1,0:T(8,128)(2,1)S(1)}, u32[]{:S(2)}, u32[]{:S(2)}) collective-permute-start(bf16[1152,512]{1,0:T(8,128)(2,1)S(1)} %convolution_convert_fusion.6), channel_id=1, source_target_pairs={{0,16},{4,20},{8,24},{12,28},{16,0},{20,4},{24,8},{28,12},{1,17},{... | collective-permute-start | bytes 3538952 | tf_op jit(solution)/shard_map/ppermute | solution.py:512
  106.1 27.8 %collective-permute-start.18 = (bf16[1152,512]{1,0:T(8,128)(2,1)S(1)}, bf16[1152,512]{1,0:T(8,128)(2,1)S(1)}, u32[]{:S(2)}, u32[]{:S(2)}) collective-permute-start(bf16[1152,512]{1,0:T(8,128)(2,1)S(1)} %convolution_convert_fusion.7), channel_id=1, source_target_pairs={{0,8},{4,12},{8,0},{12,4},{16,24},{20,28},{24,16},{28,20},{1,9},{5... | collective-permute-start | bytes 3538952 | tf_op jit(solution)/shard_map/ppermute | solution.py:512
  112.3 27.8 %collective-permute-start.17 = (bf16[1152,512]{1,0:T(8,128)(2,1)S(1)}, bf16[1152,512]{1,0:T(8,128)(2,1)S(1)}, u32[]{:S(2)}, u32[]{:S(2)}) collective-permute-start(bf16[1152,512]{1,0:T(8,128)(2,1)S(1)} %share.4), channel_id=1, source_target_pairs={{0,1},{1,0},{2,3},{3,2},{4,5},{5,4},{6,7},{7,6},{8,9},{9,8},{10,11... | collective-permute-start | bytes 3538952 | tf_op jit(solution)/shard_map/ppermute | solution.py:512
  133.8 27.1 %collective-permute-start.22 = (bf16[1152,512]{1,0:T(8,128)(2,1)}, bf16[1152,512]{1,0:T(8,128)(2,1)}, u32[]{:S(2)}, u32[]{:S(2)}) collective-permute-start(bf16[1152,512]{1,0:T(8,128)(2,1)} %convolution_convert_fusion.5), channel_id=1, source_target_pairs={{0,8},{4,12},{8,0},{12,4},{16,24},{20,28},{24,16},{28,20},{1,9},{5... | collective-permute-start | bytes 3538952 | tf_op jit(solution)/shard_map/ppermute | solution.py:512
  134.4 26.8 %collective-permute-start.23 = (bf16[1152,512]{1,0:T(8,128)(2,1)}, bf16[1152,512]{1,0:T(8,128)(2,1)}, u32[]{:S(2)}, u32[]{:S(2)}) collective-permute-start(bf16[1152,512]{1,0:T(8,128)(2,1)} %convolution_convert_fusion.4), channel_id=1, source_target_pairs={{0,16},{4,20},{8,24},{12,28},{16,0},{20,4},{24,8},{28,12},{1,17},{... | collective-permute-start | bytes 3538952 | tf_op jit(solution)/shard_map/ppermute | solution.py:512
  141.4 21.9 %collective-permute-start.21 = (bf16[1152,512]{1,0:T(8,128)(2,1)}, bf16[1152,512]{1,0:T(8,128)(2,1)}, u32[]{:S(2)}, u32[]{:S(2)}) collective-permute-start(bf16[1152,512]{1,0:T(8,128)(2,1)} %add_convert_fusion.1), channel_id=1, source_target_pairs={{0,4},{1,2},{2,1},{3,7},{4,0},{5,6},{6,5},{7,3},{8,12},{9,10},{10,... | collective-permute-start | bytes 3538952 | tf_op jit(solution)/shard_map/ppermute | solution.py:522
  141.4 28.5 %collective-permute-start.20 = (bf16[1152,512]{1,0:T(8,128)(2,1)S(1)}, bf16[1152,512]{1,0:T(8,128)(2,1)}, u32[]{:S(2)}, u32[]{:S(2)}) collective-permute-start(bf16[1152,512]{1,0:T(8,128)(2,1)S(1)} %share.5), channel_id=1, source_target_pairs={{0,1},{1,0},{2,3},{3,2},{4,5},{5,4},{6,7},{7,6},{8,9},{9,8},{10,11... | collective-permute-start | bytes 3538952 | tf_op jit(solution)/shard_map/ppermute | solution.py:512
  161.2 25.6 %collective-permute-start.26 = (bf16[1152,512]{1,0:T(8,128)(2,1)S(1)}, bf16[1152,512]{1,0:T(8,128)(2,1)S(1)}, u32[]{:S(2)}, u32[]{:S(2)}) collective-permute-start(bf16[1152,512]{1,0:T(8,128)(2,1)S(1)} %fusion.11), channel_id=1, source_target_pairs={{0,16},{4,20},{8,24},{12,28},{16,0},{20,4},{24,8},{28,12},{1,17},{... | collective-permute-start | bytes 3538952 | tf_op jit(solution)/shard_map/ppermute | solution.py:512
  162.6 25.3 %collective-permute-start.27 = (bf16[1152,512]{1,0:T(8,128)(2,1)S(1)}, bf16[1152,512]{1,0:T(8,128)(2,1)S(1)}, u32[]{:S(2)}, u32[]{:S(2)}) collective-permute-start(bf16[1152,512]{1,0:T(8,128)(2,1)S(1)} %fusion.8), channel_id=1, source_target_pairs={{0,8},{4,12},{8,0},{12,4},{16,24},{20,28},{24,16},{28,20},{1,9},{5... | collective-permute-start | bytes 3538952 | tf_op jit(solution)/shard_map/ppermute | solution.py:512
  171.6 20.4 %collective-permute-start.25 = (bf16[1152,512]{1,0:T(8,128)(2,1)S(1)}, bf16[1152,512]{1,0:T(8,128)(2,1)S(1)}, u32[]{:S(2)}, u32[]{:S(2)}) collective-permute-start(bf16[1152,512]{1,0:T(8,128)(2,1)S(1)} %add_convert_fusion), channel_id=1, source_target_pairs={{0,4},{1,2},{2,1},{3,7},{4,0},{5,6},{6,5},{7,3},{8,12},{9,10},{10,... | collective-permute-start | bytes 3538952 | tf_op jit(solution)/shard_map/ppermute | solution.py:522
  171.8 29.2 %collective-permute-start.24 = (bf16[1152,512]{1,0:T(8,128)(2,1)S(1)}, bf16[1152,512]{1,0:T(8,128)(2,1)S(1)}, u32[]{:S(2)}, u32[]{:S(2)}) collective-permute-start(bf16[1152,512]{1,0:T(8,128)(2,1)S(1)} %broadcast_select_fusion.1), channel_id=1, source_target_pairs={{0,1},{1,0},{2,3},{3,2},{4,5},{5,4},{6,7},{7,6},{8,9},{9,8},{10,11... | collective-permute-start | bytes 3538952 | tf_op jit(solution)/shard_map/ppermute | solution.py:512
  188.2 14.3 %collective-permute-start.28 = (bf16[576,1024]{1,0:T(8,128)(2,1)S(1)}, bf16[576,1024]{1,0:T(8,128)(2,1)S(1)}, u32[]{:S(2)}, u32[]{:S(2)}) collective-permute-start(bf16[576,1024]{1,0:T(8,128)(2,1)S(1)} %add_up.1), channel_id=1, source_target_pairs={{0,4},{4,0},{8,12},{12,8},{16,20},{20,16},{24,28},{28,24},{1,5},{5... | collective-permute-start | bytes 3538952 | tf_op jit(solution)/shard_map/ppermute | solution.py:512
  (33 other events, 230.9 us)

commit v2 on v1

--- a/solution.py
+++ b/solution.py
@@ -703,12 +703,13 @@
     left_out = (wide(left_of(2, lined_q)) + wide(left3)).astype(bf)
     right_out = (wide(left_of(1, lined_kv)) + wide(right3)).astype(bf)
     third = share(order, 2, xq, xkv, w_query, w_key, w_value, block_width)
+    fourth = share(order, 3, xq, xkv, w_query, w_key, w_value, block_width)
     left1, right2, left_out, right_out, lined_q, lined_kv, xq = lax.optimization_barrier(
         (left1, right2, left_out, right_out, lined_q, lined_kv, xq)
     )
     left_last, right_last = swap(left_out, "seq", 4), swap(right_out, "seq", 2)
-    second_in, first_mid, third, left_out, right_out, lined_q, lined_kv, xq = lax.optimization_barrier(
-        (second_in, first_mid, third, left_out, right_out, lined_q, lined_kv, xq)
+    second_in, first_mid, third, fourth, left_out, right_out, lined_q, lined_kv = lax.optimization_barrier(
+        (second_in, first_mid, third, fourth, left_out, right_out, lined_q, lined_kv)
     )
     inner = (level == 1) | (level == 2)
     third_in = swap(jnp.where(inner, first_mid, third), "head", 1)
@@ -716,7 +717,6 @@
     left_sum = (wide(left_of(0, lined_q)) + wide(left1)).astype(bf)
     right_sum = (wide(left_of(0, lined_kv)) + wide(right2)).astype(bf)
     cross = swap(add_up(left_sum, left_last, right_sum, right_last), "seq", 1)
-    fourth = share(order, 3, xq, xkv, w_query, w_key, w_value, block_width)
     grad_x = lay_down(fourth, third_in, jnp.where(inner, second_mid, first_in))
     grad_wq, grad_wk, grad_wv = finish(place, left_sum, left_last, right_sum, right_last, cross)
     return (grad_x, grad_wq, grad_wk, grad_wv)

time: 206 us -> 211 us (1.024)
  Pallas kernels: 61.6 us -> 69 us
  waiting for transfers between devices: 77 us -> 73.2 us
    pallas_call x1, Pallas kernels: 23.9 us -> 31.4 us  [attention(): pl.pallas_call(functools.partial(attention_kernel, n, rows, score_scale),...]
    ppermute x27, waiting for transfers between devices: 77 us -> 73.2 us  [swap(): return lax.ppermute(value, axis, [(i, i ^ by) for i in range(size)])]
    unnamed x72 -> x58, local copies, waits for them, and re-layouts: 14.7 us -> 15.1 us
  transfers between devices with their start and end apart: 29 -> 29, of which waited for: 18 -> 18; matrix products, arithmetic and copies ran while one was open for 11% -> 11% of each run, Pallas kernels for 17% -> 16%
where the time goes in v2:
time: 211 us; the launch traced here: 210 us
  waiting for transfers between devices  73.2 us (35%)
  Pallas kernels  69 us (33%)
  starting transfers between devices  29.3 us (14%)
  local copies, waits for them, and re-layouts  16.5 us (8%)
  matrix products  15.8 us (7%)
  other arithmetic  4.88 us (2%)
    ppermute x27, waiting for transfers between devices, swap(): return lax.ppermute(value, axis, [(i, i ^ by) for i in range(size)])  73.2 us
    pallas_call x1, Pallas kernels, attention(): pl.pallas_call(functools.partial(attention_kernel, n, rows, score_scale),...  31.4 us
    ppermute x27, starting transfers between devices, swap(): return lax.ppermute(value, axis, [(i, i ^ by) for i in range(size)])  29.2 us
    dot_general x8, matrix products, left_of(): jnp.dot(strips[m], lined, preferred_element_type=jnp.float32).astype(bf)  15.8 us
    unnamed x58, local copies, waits for them, and re-layouts  15.1 us
    pallas_call x4, Pallas kernels, share(): pl.pallas_call(share_kernel, out_shape=jax.ShapeDtypeStruct((width, rows)...  14.2 us
    pallas_call x4, Pallas kernels, turn(): pl.pallas_call(turn_kernel, out_shape=jax.ShapeDtypeStruct((strip, 2 * ro...  11.7 us
    pallas_call x1, Pallas kernels, pack(): pl.pallas_call(pack_kernel, out_shape=[jax.ShapeDtypeStruct((rows, 6 * HD...  4.57 us
  transfers between devices with their start and end apart: 29, of which 18 were waited for; matrix products, arithmetic and copies ran while one was open for 11% of the time, Pallas kernels for 16%

profile of v2, /device:TPU:0, one launch (start us, length us, event | category | flops | bytes accessed | tf_op | source)
XLA Modules:
  0.0 209.9 jit_solution(6899998393053021400)
XLA Ops:
  2.5 4.6 %pack.1 = (bf16[512,768]{1,0:T(8,128)(2,1)}, bf16[512,768]{1,0:T(8,128)(2,1)}, bf16[512,768]{1,0:T(8,128)(2,1)}, bf16[512,768]{1,0:T(8,128)(2,1)}) custom-call(s32[9]{0:T(128)} %stack.36.place, bf16[512,1024]{1,0:T(8,128)(2,1)} %q.1, bf16[512,512]{1,0:T(8,128)(2,1)} %k.1, bf16[512,512]{1,0:T(8,128)(2,1)} %v.1, bf16[512,1024]{1,0:T(8,128)(2,1)} %g.1), custom_call_target="tpu_custom_call" | custom-call | tf_op jit(solution)/shard_map/pack/pallas_call | solution.py:424
  7.0 3.5 %collective-permute-start.3 = (bf16[512,768]{1,0:T(8,128)(2,1)}, bf16[512,768]{1,0:T(8,128)(2,1)S(1)}, u32[]{:S(2)}, u32[]{:S(2)}) collective-permute-start(bf16[512,768]{1,0:T(8,128)(2,1)} %get-tuple-element.93), channel_id=1, source_target_pairs={{0,24},{4,28},{8,16},{12,20},{16,8},{20,12},{24,0},{28,4},{1,25},{... | collective-permute-start | bytes 2359304 | tf_op jit(solution)/shard_map/ppermute | solution.py:512
  11.2 2.3 %copy-done.1 = bf16[512,4608]{1,0:T(8,128)(2,1)S(1)} copy-done((bf16[512,4608]{1,0:T(8,128)(2,1)S(1)}, bf16[512,4608]{1,0:T(8,128)(2,1)}, u32[]{:S(2)}) %copy-start.1) | copy-done | bytes 4718616
  13.6 2.8 %turn.6 = bf16[1152,1024]{1,0:T(8,128)(2,1)S(1)} custom-call(s32[9]{0:T(128)S(1)} %copy-done.14, bf16[512,4608]{1,0:T(8,128)(2,1)S(1)} %copy-done.1, bf16[512,4608]{1,0:T(8,128)(2,1)} %collective-permute-done.peer), custom_call_target="tpu_custom_call" | custom-call | tf_op jit(solution)/shard_map/turn/pallas_call | solution.py:550
  17.8 2.8 %turn.5 = bf16[1152,1024]{1,0:T(8,128)(2,1)S(1)} custom-call(s32[9]{0:T(128)S(1)} %copy-done.14, bf16[512,4608]{1,0:T(8,128)(2,1)S(1)} %copy-done.1, bf16[512,4608]{1,0:T(8,128)(2,1)} %collective-permute-done.peer), custom_call_target="tpu_custom_call" | custom-call | tf_op jit(solution)/shard_map/turn/pallas_call | solution.py:550
  22.0 3.1 %turn.4 = bf16[1152,1024]{1,0:T(8,128)(2,1)S(1)} custom-call(s32[9]{0:T(128)S(1)} %copy-done.14, bf16[512,4608]{1,0:T(8,128)(2,1)S(1)} %copy-done.1, bf16[512,4608]{1,0:T(8,128)(2,1)} %collective-permute-done.peer), custom_call_target="tpu_custom_call" | custom-call | tf_op jit(solution)/shard_map/turn/pallas_call | solution.py:550
  26.6 2.6 %collective-permute-done.3.refs_3_ = bf16[512,768]{1,0:T(8,128)(2,1)S(1)} collective-permute-done((bf16[512,768]{1,0:T(8,128)(2,1)}, bf16[512,768]{1,0:T(8,128)(2,1)S(1)}, u32[]{:S(2)}, u32[]{:S(2)}) %collective-permute-start.3) | collective-permute-done | bytes 786464 | tf_op jit(solution)/shard_map/ppermute | solution.py:512
  29.2 16.6 %collective-permute-done.2.refs_2_ = bf16[512,768]{1,0:T(8,128)(2,1)S(1)} collective-permute-done((bf16[512,768]{1,0:T(8,128)(2,1)}, bf16[512,768]{1,0:T(8,128)(2,1)S(1)}, u32[]{:S(2)}, u32[]{:S(2)}) %collective-permute-start.2) | collective-permute-done | bytes 786464 | tf_op jit(solution)/shard_map/ppermute | solution.py:512
  49.2 31.4 %attention.1 = (bf16[4096,128]{1,0:T(8,128)(2,1)S(1)}, f32[4096,128]{1,0:T(8,128)S(1)}, bf16[4096,128]{1,0:T(8,128)(2,1)S(1)}) custom-call(s32[9]{0:T(128)S(1)} %copy-done.14, s32[8]{0:T(128)S(1)} %copy-done.16, bf16[512,768]{1,0:T(8,128)(2,1)S(1)} %copy-done.15, bf16[512,768]{1,0:T(8,128)(2,1)S(1)} %collective-permute-done.1.refs_1_, ...), custom_call_target="tpu_custom_call" | custom-call | flops 25769803776 | bytes 8388608 | tf_op jit(solution)/shard_map/attention/pallas_call | solution.py:361
  80.9 1.9 collective-permute-start.10
  88.0 8.9 %collective-permute-done.8.refs_1_ = bf16[1024,128]{1,0:T(8,128)(2,1)S(1)} collective-permute-done((bf16[1024,128]{1,0:T(8,128)(2,1)S(1)}, bf16[1024,128]{1,0:T(8,128)(2,1)S(1)}, u32[]{:S(2)}, u32[]{:S(2)}) %collective-permute-start.8) | collective-permute-done | bytes 262176 | tf_op jit(solution)/shard_map/ppermute | solution.py:512
  97.6 3.0 %turn.7 = bf16[1152,1024]{1,0:T(8,128)(2,1)S(1)} custom-call(s32[9]{0:T(128)S(1)} %copy-done.14, bf16[512,4608]{1,0:T(8,128)(2,1)S(1)} %bitcast.31, bf16[512,4608]{1,0:T(8,128)(2,1)} %collective-permute-done.peer), custom_call_target="tpu_custom_call" | custom-call | tf_op jit(solution)/shard_map/turn/pallas_call | solution.py:550
  102.4 5.0 %collective-permute-done.13.refs_6_ = bf16[1024,128]{1,0:T(8,128)(2,1)S(1)} collective-permute-done((bf16[1024,128]{1,0:T(8,128)(2,1)S(1)}, bf16[1024,128]{1,0:T(8,128)(2,1)S(1)}, u32[]{:S(2)}, u32[]{:S(2)}) %collective-permute-start.13) | collective-permute-done | bytes 262176 | tf_op jit(solution)/shard_map/ppermute | solution.py:512
  109.3 2.4 %convolution_convert_fusion.6 = bf16[1152,512]{1,0:T(8,128)(2,1)} fusion(bf16[1152,1024]{1,0:T(8,128)(2,1)S(1)} %turn.7, bf16[1024,512]{1,0:T(8,128)(2,1)S(1)} %get-tuple-element.159.mine), kind=kOutput, calls=%fused_computation.18 | convolution fusion | flops 1208549376 | bytes 4587520 | tf_op jit(solution)/shard_map/dot_general | solution.py:680
  113.1 2.4 %convolution_convert_fusion.7 = bf16[1152,512]{1,0:T(8,128)(2,1)} fusion(bf16[1152,1024]{1,0:T(8,128)(2,1)S(1)} %turn.7, bf16[1024,512]{1,0:T(8,128)(2,1)S(1)} %get-tuple-element.157.mine), kind=kOutput, calls=%fused_computation.19 | convolution fusion | flops 1208549376 | bytes 4587520 | tf_op jit(solution)/shard_map/dot_general | solution.py:680
  118.0 3.5 %share.4 = bf16[1152,512]{1,0:T(8,128)(2,1)S(1)} custom-call(s32[4]{0:T(128)S(1)} %dynamic-slice_bitcast_fusion.order, bf16[1024,512]{1,0:T(8,128)(2,1)S(1)} %stand_up.2.xq, bf16[1024,512]{1,0:T(8,128)(2,1)S(1)} %stand_up.3.xkv, bf16[4608,1024]{1,0:T(8,128)(2,1)S(1)} %bitcast.27, bf16[4608,512]{1,0:T(8,128)(2,1)S(1)} %bitcast.33, bf16[4608,512]{1,0:T(8,128)(2,1)S(1)} %bitcast.35), custom_call_target="tpu_custom_call" | custom-call | flops 2415919104 | bytes 4718592 | tf_op jit(solution)/shard_map/share/pallas_call | solution.py:606
  123.4 3.7 %copy-done = bf16[4608,1024]{1,0:T(8,128)(2,1)S(1)} copy-done((bf16[4608,1024]{1,0:T(8,128)(2,1)S(1)}, bf16[4608,1024]{1,0:T(8,128)(2,1)}, u32[]{:S(2)}) %copy-start) | copy-done | bytes 9437208
  127.0 2.3 %copy-done.2 = bf16[4608,512]{1,0:T(8,128)(2,1)S(1)} copy-done((bf16[4608,512]{1,0:T(8,128)(2,1)S(1)}, bf16[4608,512]{1,0:T(8,128)(2,1)}, u32[]{:S(2)}) %copy-start.2) | copy-done | bytes 4718616
  129.4 2.3 %copy-done.3 = bf16[4608,512]{1,0:T(8,128)(2,1)S(1)} copy-done((bf16[4608,512]{1,0:T(8,128)(2,1)S(1)}, bf16[4608,512]{1,0:T(8,128)(2,1)}, u32[]{:S(2)}) %copy-start.3) | copy-done | bytes 4718616
  131.7 3.5 %share.5 = bf16[1152,512]{1,0:T(8,128)(2,1)S(1)} custom-call(s32[4]{0:T(128)S(1)} %dynamic-slice_bitcast_fusion.order, bf16[1024,512]{1,0:T(8,128)(2,1)S(1)} %stand_up.2.xq, bf16[1024,512]{1,0:T(8,128)(2,1)S(1)} %stand_up.3.xkv, bf16[4608,1024]{1,0:T(8,128)(2,1)S(1)} %copy-done, bf16[4608,512]{1,0:T(8,128)(2,1)S(1)} %copy-done.2, bf16[4608,512]{1,0:T(8,128)(2,1)S(1)} %copy-done.3), custom_call_target="tpu_custom_call" | custom-call | flops 2415919104 | bytes 4718592 | tf_op jit(solution)/shard_map/share/pallas_call | solution.py:606
  140.0 3.5 %collective-permute-done.18 = bf16[1152,512]{1,0:T(8,128)(2,1)} collective-permute-done((bf16[1152,512]{1,0:T(8,128)(2,1)}, bf16[1152,512]{1,0:T(8,128)(2,1)}, u32[]{:S(2)}, u32[]{:S(2)}) %collective-permute-start.18) | collective-permute-done | bytes 1179680 | tf_op jit(solution)/shard_map/ppermute | solution.py:512
  145.5 3.6 %collective-permute-done.17 = bf16[1152,512]{1,0:T(8,128)(2,1)} collective-permute-done((bf16[1152,512]{1,0:T(8,128)(2,1)S(1)}, bf16[1152,512]{1,0:T(8,128)(2,1)}, u32[]{:S(2)}, u32[]{:S(2)}) %collective-permute-start.17) | collective-permute-done | bytes 1179680 | tf_op jit(solution)/shard_map/ppermute | solution.py:512
  152.6 3.5 %share.7.a = bf16[1152,512]{1,0:T(8,128)(2,1)S(1)} custom-call(s32[4]{0:T(128)S(1)} %dynamic-slice_bitcast_fusion.order, bf16[1024,512]{1,0:T(8,128)(2,1)S(1)} %stand_up.2.xq, bf16[1024,512]{1,0:T(8,128)(2,1)S(1)} %stand_up.3.xkv, bf16[4608,1024]{1,0:T(8,128)(2,1)S(1)} %bitcast.29, bf16[4608,512]{1,0:T(8,128)(2,1)S(1)} %copy-done.2, ...), custom_call_target="tpu_custom_call" | custom-call | flops 2415919104 | bytes 4718592 | tf_op jit(solution)/shard_map/share/pallas_call | solution.py:606
  156.1 3.5 %share.6 = bf16[1152,512]{1,0:T(8,128)(2,1)S(1)} custom-call(s32[4]{0:T(128)S(1)} %dynamic-slice_bitcast_fusion.order, bf16[1024,512]{1,0:T(8,128)(2,1)S(1)} %stand_up.2.xq, bf16[1024,512]{1,0:T(8,128)(2,1)S(1)} %stand_up.3.xkv, bf16[4608,1024]{1,0:T(8,128)(2,1)S(1)} %bitcast.29, bf16[4608,512]{1,0:T(8,128)(2,1)S(1)} %copy-done.2, ...), custom_call_target="tpu_custom_call" | custom-call | flops 2415919104 | bytes 4718592 | tf_op jit(solution)/shard_map/share/pallas_call | solution.py:606
  159.7 2.7 %fusion.8 = bf16[1152,512]{1,0:T(8,128)(2,1)S(1)} fusion(bf16[1152,1024]{1,0:T(8,128)(2,1)S(1)} %copy-done.9, bf16[1024,512]{1,0:T(8,128)(2,1)S(1)} %copy-done.13, bf16[1152,512]{1,0:T(8,128)(2,1)} %collective-permute-done.19), kind=kOutput, calls=%fused_computation.11 | convolution fusion | flops 1210908672 | bytes 5767168 | tf_op jit(solution)/shard_map/dot_general | solution.py:680
  162.4 2.7 %fusion.11 = bf16[1152,512]{1,0:T(8,128)(2,1)S(1)} fusion(bf16[1152,1024]{1,0:T(8,128)(2,1)S(1)} %copy-done.7, bf16[1024,512]{1,0:T(8,128)(2,1)S(1)} %copy-done.11, bf16[1152,512]{1,0:T(8,128)(2,1)} %collective-permute-done.18), kind=kOutput, calls=%fused_computation.15 | convolution fusion | flops 1210908672 | bytes 5767168 | tf_op jit(solution)/shard_map/dot_general | solution.py:680
  165.0 5.3 %collective-permute-done.22 = bf16[1152,512]{1,0:T(8,128)(2,1)S(1)} collective-permute-done((bf16[1152,512]{1,0:T(8,128)(2,1)S(1)}, bf16[1152,512]{1,0:T(8,128)(2,1)S(1)}, u32[]{:S(2)}, u32[]{:S(2)}) %collective-permute-start.22) | collective-permute-done | bytes 1179680 | tf_op jit(solution)/shard_map/ppermute | solution.py:512
  172.7 2.9 %collective-permute-done.20 = bf16[1152,512]{1,0:T(8,128)(2,1)S(1)} collective-permute-done((bf16[1152,512]{1,0:T(8,128)(2,1)S(1)}, bf16[1152,512]{1,0:T(8,128)(2,1)S(1)}, u32[]{:S(2)}, u32[]{:S(2)}) %collective-permute-start.20) | collective-permute-done | bytes 1179680 | tf_op jit(solution)/shard_map/ppermute | solution.py:512
  176.2 6.3 %collective-permute-start.24 = (bf16[1152,512]{1,0:T(8,128)(2,1)S(1)}, bf16[1152,512]{1,0:T(8,128)(2,1)S(1)}, u32[]{:S(2)}, u32[]{:S(2)}) collective-permute-start(bf16[1152,512]{1,0:T(8,128)(2,1)S(1)} %broadcast_select_fusion.1), channel_id=1, source_target_pairs={{0,1},{1,0},{2,3},{3,2},{4,5},{5,4},{6,7},{7,6},{8,9},{9,8},{10,11... | collective-permute-start | bytes 3538952 | tf_op jit(solution)/shard_map/ppermute | solution.py:512
  185.3 10.9 %collective-permute-done.26.left_last = bf16[1152,512]{1,0:T(8,128)(2,1)S(1)} collective-permute-done((bf16[1152,512]{1,0:T(8,128)(2,1)S(1)}, bf16[1152,512]{1,0:T(8,128)(2,1)S(1)}, u32[]{:S(2)}, u32[]{:S(2)}) %collective-permute-start.26) | collective-permute-done | bytes 1179680 | tf_op jit(solution)/shard_map/ppermute | solution.py:512
  199.2 6.6 %collective-permute-done.24.b = bf16[1152,512]{1,0:T(8,128)(2,1)S(1)} collective-permute-done((bf16[1152,512]{1,0:T(8,128)(2,1)S(1)}, bf16[1152,512]{1,0:T(8,128)(2,1)S(1)}, u32[]{:S(2)}, u32[]{:S(2)}) %collective-permute-start.24) | collective-permute-done | bytes 1179680 | tf_op jit(solution)/shard_map/ppermute | solution.py:512
  207.3 2.6 %finish.1 = (bf16[576,1024]{1,0:T(8,128)(2,1)}, bf16[576,512]{1,0:T(8,128)(2,1)}, bf16[576,512]{1,0:T(8,128)(2,1)}) custom-call(s32[9]{0:T(128)S(1)} %copy-done.14, bf16[1152,512]{1,0:T(8,128)(2,1)S(1)} %fusion.5.left, bf16[1152,512]{1,0:T(8,128)(2,1)S(1)} %collective-permute-done.26.left_last, bf16[1152,512]{1,0:T(8,128)(2,1)S(1)} %fusion.2.right, ...), custom_call_target="tpu_custom_call" | custom-call | tf_op jit(solution)/shard_map/finish/pallas_call | solution.py:500
  (127 shorter events, 45.7 us)
Async XLA Ops:
  0.6 10.6 %collective-permute-start = (bf16[512,4608]{1,0:T(8,128)(2,1)}, bf16[512,4608]{1,0:T(8,128)(2,1)}, u32[]{:S(2)}, u32[]{:S(2)}) collective-permute-start(bf16[512,4608]{1,0:T(8,128)(2,1)} %own.3), channel_id=1, source_target_pairs={{0,4},{4,0},{8,12},{12,8},{16,20},{20,16},{24,28},{28,24},{1,5},{5... | collective-permute-start | bytes 14155784 | tf_op jit(solution)/shard_map/ppermute | solution.py:512
  7.0 22.2 %collective-permute-start.3 = (bf16[512,768]{1,0:T(8,128)(2,1)}, bf16[512,768]{1,0:T(8,128)(2,1)S(1)}, u32[]{:S(2)}, u32[]{:S(2)}) collective-permute-start(bf16[512,768]{1,0:T(8,128)(2,1)} %get-tuple-element.93), channel_id=1, source_target_pairs={{0,24},{4,28},{8,16},{12,20},{16,8},{20,12},{24,0},{28,4},{1,25},{... | collective-permute-start | bytes 2359304 | tf_op jit(solution)/shard_map/ppermute | solution.py:512
  10.6 35.3 %collective-permute-start.2 = (bf16[512,768]{1,0:T(8,128)(2,1)}, bf16[512,768]{1,0:T(8,128)(2,1)S(1)}, u32[]{:S(2)}, u32[]{:S(2)}) collective-permute-start(bf16[512,768]{1,0:T(8,128)(2,1)} %get-tuple-element.91), channel_id=1, source_target_pairs={{0,16},{4,20},{8,24},{12,28},{16,0},{20,4},{24,8},{28,12},{1,17},{... | collective-permute-start | bytes 2359304 | tf_op jit(solution)/shard_map/ppermute | solution.py:512
  11.1 35.0 %collective-permute-start.1 = (bf16[512,768]{1,0:T(8,128)(2,1)}, bf16[512,768]{1,0:T(8,128)(2,1)S(1)}, u32[]{:S(2)}, u32[]{:S(2)}) collective-permute-start(bf16[512,768]{1,0:T(8,128)(2,1)} %get-tuple-element.89), channel_id=1, source_target_pairs={{0,8},{4,12},{8,0},{12,4},{16,24},{20,28},{24,16},{28,20},{1,9},{5... | collective-permute-start | bytes 2359304 | tf_op jit(solution)/shard_map/ppermute | solution.py:512
  11.2 36.3 %collective-permute-start.4 = (bf16[512,768]{1,0:T(8,128)(2,1)}, bf16[512,768]{1,0:T(8,128)(2,1)S(1)}, u32[]{:S(2)}, u32[]{:S(2)}) collective-permute-start(bf16[512,768]{1,0:T(8,128)(2,1)} %get-tuple-element.101.refs_0_), channel_id=1, source_target_pairs={{0,4},{4,0},{8,12},{12,8},{16,20},{20,16},{24,28},{28,24},{1,5},{5... | collective-permute-start | bytes 2359304 | tf_op jit(solution)/shard_map/ppermute | solution.py:512
  22.0 27.2 %copy-start.16 = (s32[8]{0:T(128)S(1)}, s32[8]{0:T(128)}, u32[]{:S(2)}) copy-start(s32[8]{0:T(128)} %lens.1) | copy-start | bytes 100
  22.0 75.6 %slice-start.6 = ((s8[4718592]{0:T(1024)(128)(4,1)}), s8[4194304]{0:T(1024)(128)(4,1)S(1)}, s32[]{:S(2)}) async-start(s8[4718592]{0:T(1024)(128)(4,1)} %bitcast.30), calls=%async_computation.6 | async-start | bytes 8388608
  29.2 18.3 %collective-permute-start.7 = (bf16[512,768]{1,0:T(8,128)(2,1)S(1)}, bf16[512,768]{1,0:T(8,128)(2,1)S(1)}, u32[]{:S(2)}, u32[]{:S(2)}) collective-permute-start(bf16[512,768]{1,0:T(8,128)(2,1)S(1)} %collective-permute-done.3.refs_3_), channel_id=1, source_target_pairs={{0,4},{4,0},{8,12},{12,8},{16,20},{20,16},{24,28},{28,24},{1,5},{5... | collective-permute-start | bytes 2359304 | tf_op jit(solution)/shard_map/ppermute | solution.py:512
  45.8 2.3 %collective-permute-start.6 = (bf16[512,768]{1,0:T(8,128)(2,1)S(1)}, bf16[512,768]{1,0:T(8,128)(2,1)S(1)}, u32[]{:S(2)}, u32[]{:S(2)}) collective-permute-start(bf16[512,768]{1,0:T(8,128)(2,1)S(1)} %collective-permute-done.2.refs_2_), channel_id=1, source_target_pairs={{0,4},{4,0},{8,12},{12,8},{16,20},{20,16},{24,28},{28,24},{1,5},{5... | collective-permute-start | bytes 2359304 | tf_op jit(solution)/shard_map/ppermute | solution.py:512
  46.1 3.1 %collective-permute-start.5 = (bf16[512,768]{1,0:T(8,128)(2,1)S(1)}, bf16[512,768]{1,0:T(8,128)(2,1)S(1)}, u32[]{:S(2)}, u32[]{:S(2)}) collective-permute-start(bf16[512,768]{1,0:T(8,128)(2,1)S(1)} %collective-permute-done.1.refs_1_), channel_id=1, source_target_pairs={{0,4},{4,0},{8,12},{12,8},{16,20},{20,16},{24,28},{28,24},{1,5},{5... | collective-permute-start | bytes 2359304 | tf_op jit(solution)/shard_map/ppermute | solution.py:512
  49.2 48.4 %slice-start.7 = ((s8[4718592]{0:T(1024)(128)(4,1)}), s8[524288]{0:T(1024)(128)(4,1)S(1)}, s32[]{:S(2)}) async-start(s8[4718592]{0:T(1024)(128)(4,1)} %bitcast.30), calls=%async_computation.7 | async-start | bytes 1048576
  80.7 3.8 %collective-permute-start.11 = (bf16[4096,128]{1,0:T(8,128)(2,1)S(1)}, bf16[4096,128]{1,0:T(8,128)(2,1)S(1)}, u32[]{:S(2)}, u32[]{:S(2)}) collective-permute-start(bf16[4096,128]{1,0:T(8,128)(2,1)S(1)} %get-tuple-element.114), channel_id=1, source_target_pairs={{0,4},{4,0},{8,12},{12,8},{16,20},{20,16},{24,28},{28,24},{1,5},{5... | collective-permute-start | bytes 3145736 | tf_op jit(solution)/shard_map/ppermute | solution.py:512
  80.9 19.7 %collective-permute-start.10 = (bf16[1024,128]{1,0:T(8,128)(2,1)S(1)}, bf16[1024,128]{1,0:T(8,128)(2,1)S(1)}, u32[]{:S(2)}, u32[]{:S(2)}) collective-permute-start(bf16[1024,128]{1,0:T(8,128)(2,1)S(1)} %get-tuple-element.168), channel_id=1, source_target_pairs={{0,24},{4,28},{8,16},{12,20},{16,8},{20,12},{24,0},{28,4},{1,25},{... | collective-permute-start | bytes 786440 | tf_op jit(solution)/shard_map/ppermute | solution.py:512
  82.8 17.8 %collective-permute-start.9 = (bf16[1024,128]{1,0:T(8,128)(2,1)S(1)}, bf16[1024,128]{1,0:T(8,128)(2,1)S(1)}, u32[]{:S(2)}, u32[]{:S(2)}) collective-permute-start(bf16[1024,128]{1,0:T(8,128)(2,1)S(1)} %get-tuple-element.169), channel_id=1, source_target_pairs={{0,16},{4,20},{8,24},{12,28},{16,0},{20,4},{24,8},{28,12},{1,17},{... | collective-permute-start | bytes 786440 | tf_op jit(solution)/shard_map/ppermute | solution.py:512
  84.2 12.8 %collective-permute-start.8 = (bf16[1024,128]{1,0:T(8,128)(2,1)S(1)}, bf16[1024,128]{1,0:T(8,128)(2,1)S(1)}, u32[]{:S(2)}, u32[]{:S(2)}) collective-permute-start(bf16[1024,128]{1,0:T(8,128)(2,1)S(1)} %get-tuple-element.171), channel_id=1, source_target_pairs={{0,8},{4,12},{8,0},{12,4},{16,24},{20,28},{24,16},{28,20},{1,9},{5... | collective-permute-start | bytes 786440 | tf_op jit(solution)/shard_map/ppermute | solution.py:512
  84.8 17.6 %collective-permute-start.14 = (bf16[1024,128]{1,0:T(8,128)(2,1)S(1)}, bf16[1024,128]{1,0:T(8,128)(2,1)S(1)}, u32[]{:S(2)}, u32[]{:S(2)}) collective-permute-start(bf16[1024,128]{1,0:T(8,128)(2,1)S(1)} %get-tuple-element.164), channel_id=1, source_target_pairs={{0,24},{4,28},{8,16},{12,20},{16,8},{20,12},{24,0},{28,4},{1,25},{... | collective-permute-start | bytes 786440 | tf_op jit(solution)/shard_map/ppermute | solution.py:512
  86.7 20.7 %collective-permute-start.13 = (bf16[1024,128]{1,0:T(8,128)(2,1)S(1)}, bf16[1024,128]{1,0:T(8,128)(2,1)S(1)}, u32[]{:S(2)}, u32[]{:S(2)}) collective-permute-start(bf16[1024,128]{1,0:T(8,128)(2,1)S(1)} %get-tuple-element.165), channel_id=1, source_target_pairs={{0,16},{4,20},{8,24},{12,28},{16,0},{20,4},{24,8},{28,12},{1,17},{... | collective-permute-start | bytes 786440 | tf_op jit(solution)/shard_map/ppermute | solution.py:512
  97.0 10.7 %collective-permute-start.12 = (bf16[1024,128]{1,0:T(8,128)(2,1)S(1)}, bf16[1024,128]{1,0:T(8,128)(2,1)S(1)}, u32[]{:S(2)}, u32[]{:S(2)}) collective-permute-start(bf16[1024,128]{1,0:T(8,128)(2,1)S(1)} %get-tuple-element.166), channel_id=1, source_target_pairs={{0,8},{4,12},{8,0},{12,4},{16,24},{20,28},{24,16},{28,20},{1,9},{5... | collective-permute-start | bytes 786440 | tf_op jit(solution)/shard_map/ppermute | solution.py:512
  108.7 7.4 %collective-permute-start.15 = (bf16[512,512]{1,0:T(8,128)(2,1)S(1)}, bf16[512,512]{1,0:T(8,128)(2,1)S(1)}, u32[]{:S(2)}, u32[]{:S(2)}) collective-permute-start(bf16[512,512]{1,0:T(8,128)(2,1)S(1)} %get-tuple-element.126), channel_id=1, source_target_pairs={{0,4},{4,0},{8,12},{12,8},{16,20},{20,16},{24,28},{28,24},{1,5},{5... | collective-permute-start | bytes 1572872 | tf_op jit(solution)/shard_map/ppermute | solution.py:512
  108.8 7.3 %collective-permute-start.16 = (bf16[512,512]{1,0:T(8,128)(2,1)S(1)}, bf16[512,512]{1,0:T(8,128)(2,1)S(1)}, u32[]{:S(2)}, u32[]{:S(2)}) collective-permute-start(bf16[512,512]{1,0:T(8,128)(2,1)S(1)} %get-tuple-element.127), channel_id=1, source_target_pairs={{0,4},{4,0},{8,12},{12,8},{16,20},{20,16},{24,28},{28,24},{1,5},{5... | collective-permute-start | bytes 1572872 | tf_op jit(solution)/shard_map/ppermute | solution.py:512
  111.7 28.3 %collective-permute-start.19 = (bf16[1152,512]{1,0:T(8,128)(2,1)}, bf16[1152,512]{1,0:T(8,128)(2,1)}, u32[]{:S(2)}, u32[]{:S(2)}) collective-permute-start(bf16[1152,512]{1,0:T(8,128)(2,1)} %convolution_convert_fusion.6), channel_id=1, source_target_pairs={{0,16},{4,20},{8,24},{12,28},{16,0},{20,4},{24,8},{28,12},{1,17},{... | collective-permute-start | bytes 3538952 | tf_op jit(solution)/shard_map/ppermute | solution.py:512
  115.5 28.0 %collective-permute-start.18 = (bf16[1152,512]{1,0:T(8,128)(2,1)}, bf16[1152,512]{1,0:T(8,128)(2,1)}, u32[]{:S(2)}, u32[]{:S(2)}) collective-permute-start(bf16[1152,512]{1,0:T(8,128)(2,1)} %convolution_convert_fusion.7), channel_id=1, source_target_pairs={{0,8},{4,12},{8,0},{12,4},{16,24},{20,28},{24,16},{28,20},{1,9},{5... | collective-permute-start | bytes 3538952 | tf_op jit(solution)/shard_map/ppermute | solution.py:512
  121.5 27.6 %collective-permute-start.17 = (bf16[1152,512]{1,0:T(8,128)(2,1)S(1)}, bf16[1152,512]{1,0:T(8,128)(2,1)}, u32[]{:S(2)}, u32[]{:S(2)}) collective-permute-start(bf16[1152,512]{1,0:T(8,128)(2,1)S(1)} %share.4), channel_id=1, source_target_pairs={{0,1},{1,0},{2,3},{3,2},{4,5},{5,4},{6,7},{7,6},{8,9},{9,8},{10,11... | collective-permute-start | bytes 3538952 | tf_op jit(solution)/shard_map/ppermute | solution.py:512
  143.5 26.8 %collective-permute-start.22 = (bf16[1152,512]{1,0:T(8,128)(2,1)S(1)}, bf16[1152,512]{1,0:T(8,128)(2,1)S(1)}, u32[]{:S(2)}, u32[]{:S(2)}) collective-permute-start(bf16[1152,512]{1,0:T(8,128)(2,1)S(1)} %convolution_convert_fusion.5), channel_id=1, source_target_pairs={{0,8},{4,12},{8,0},{12,4},{16,24},{20,28},{24,16},{28,20},{1,9},{5... | collective-permute-start | bytes 3538952 | tf_op jit(solution)/shard_map/ppermute | solution.py:512
  144.1 26.5 %collective-permute-start.23 = (bf16[1152,512]{1,0:T(8,128)(2,1)S(1)}, bf16[1152,512]{1,0:T(8,128)(2,1)S(1)}, u32[]{:S(2)}, u32[]{:S(2)}) collective-permute-start(bf16[1152,512]{1,0:T(8,128)(2,1)S(1)} %convolution_convert_fusion.4), channel_id=1, source_target_pairs={{0,16},{4,20},{8,24},{12,28},{16,0},{20,4},{24,8},{28,12},{1,17},{... | collective-permute-start | bytes 3538952 | tf_op jit(solution)/shard_map/ppermute | solution.py:512
  149.1 26.5 %collective-permute-start.20 = (bf16[1152,512]{1,0:T(8,128)(2,1)S(1)}, bf16[1152,512]{1,0:T(8,128)(2,1)S(1)}, u32[]{:S(2)}, u32[]{:S(2)}) collective-permute-start(bf16[1152,512]{1,0:T(8,128)(2,1)S(1)} %share.5), channel_id=1, source_target_pairs={{0,1},{1,0},{2,3},{3,2},{4,5},{5,4},{6,7},{7,6},{8,9},{9,8},{10,11... | collective-permute-start | bytes 3538952 | tf_op jit(solution)/shard_map/ppermute | solution.py:512
  152.5 20.2 %collective-permute-start.21 = (bf16[1152,512]{1,0:T(8,128)(2,1)S(1)}, bf16[1152,512]{1,0:T(8,128)(2,1)S(1)}, u32[]{:S(2)}, u32[]{:S(2)}) collective-permute-start(bf16[1152,512]{1,0:T(8,128)(2,1)S(1)} %add_convert_fusion.1), channel_id=1, source_target_pairs={{0,4},{1,2},{2,1},{3,7},{4,0},{5,6},{6,5},{7,3},{8,12},{9,10},{10,... | collective-permute-start | bytes 3538952 | tf_op jit(solution)/shard_map/ppermute | solution.py:522
  170.6 25.6 %collective-permute-start.26 = (bf16[1152,512]{1,0:T(8,128)(2,1)S(1)}, bf16[1152,512]{1,0:T(8,128)(2,1)S(1)}, u32[]{:S(2)}, u32[]{:S(2)}) collective-permute-start(bf16[1152,512]{1,0:T(8,128)(2,1)S(1)} %fusion.11), channel_id=1, source_target_pairs={{0,16},{4,20},{8,24},{12,28},{16,0},{20,4},{24,8},{28,12},{1,17},{... | collective-permute-start | bytes 3538952 | tf_op jit(solution)/shard_map/ppermute | solution.py:512
  172.0 25.3 %collective-permute-start.27 = (bf16[1152,512]{1,0:T(8,128)(2,1)S(1)}, bf16[1152,512]{1,0:T(8,128)(2,1)S(1)}, u32[]{:S(2)}, u32[]{:S(2)}) collective-permute-start(bf16[1152,512]{1,0:T(8,128)(2,1)S(1)} %fusion.8), channel_id=1, source_target_pairs={{0,8},{4,12},{8,0},{12,4},{16,24},{20,28},{24,16},{28,20},{1,9},{5... | collective-permute-start | bytes 3538952 | tf_op jit(solution)/shard_map/ppermute | solution.py:512
  175.9 21.8 %collective-permute-start.25 = (bf16[1152,512]{1,0:T(8,128)(2,1)S(1)}, bf16[1152,512]{1,0:T(8,128)(2,1)S(1)}, u32[]{:S(2)}, u32[]{:S(2)}) collective-permute-start(bf16[1152,512]{1,0:T(8,128)(2,1)S(1)} %add_convert_fusion), channel_id=1, source_target_pairs={{0,4},{1,2},{2,1},{3,7},{4,0},{5,6},{6,5},{7,3},{8,12},{9,10},{10,... | collective-permute-start | bytes 3538952 | tf_op jit(solution)/shard_map/ppermute | solution.py:522
  176.2 29.6 %collective-permute-start.24 = (bf16[1152,512]{1,0:T(8,128)(2,1)S(1)}, bf16[1152,512]{1,0:T(8,128)(2,1)S(1)}, u32[]{:S(2)}, u32[]{:S(2)}) collective-permute-start(bf16[1152,512]{1,0:T(8,128)(2,1)S(1)} %broadcast_select_fusion.1), channel_id=1, source_target_pairs={{0,1},{1,0},{2,3},{3,2},{4,5},{5,4},{6,7},{7,6},{8,9},{9,8},{10,11... | collective-permute-start | bytes 3538952 | tf_op jit(solution)/shard_map/ppermute | solution.py:512
  197.7 9.6 %collective-permute-start.28 = (bf16[576,1024]{1,0:T(8,128)(2,1)S(1)}, bf16[576,1024]{1,0:T(8,128)(2,1)S(1)}, u32[]{:S(2)}, u32[]{:S(2)}) collective-permute-start(bf16[576,1024]{1,0:T(8,128)(2,1)S(1)} %add_up.1), channel_id=1, source_target_pairs={{0,4},{4,0},{8,12},{12,8},{16,20},{20,16},{24,28},{28,24},{1,5},{5... | collective-permute-start | bytes 3538952 | tf_op jit(solution)/shard_map/ppermute | solution.py:512
  (26 other events, 179.1 us)
